TPU v7x, 32 devices: a whole 2x2x4 slice. The times are simulated.
32 devices in a mesh: dp: 16 (over z, y, x), tensor: 2 (over core).
Axes of the slice: x: 2, y: 2, z: 4, core: 2. Of those that a mesh axis runs over, the one named last changes fastest.
Arguments:
- embeds: bfloat16 [256, 4608], P('dp'), may hold values from -6 to 6
- owner: int32 [32, 8], P('dp'), may hold values from 0 to 7, each once within a row
- pairs: int32 [32, 56, 2], P('dp'), may hold values from 0 to 7, as said below
- pref_weight: bfloat16 [2, 4608, 4608], P(None, 'dp', 'tensor'), may hold values from -0.0625 to 0.0625
- pref_bias: float32 [4608], P('tensor'), may hold values from -3 to 3
- pref_out: float32 [4608], P('tensor'), may hold values from -0.375 to 0.375
- logratio: float32 [256], P('dp'), may hold values from -3 to 3
- attn_out: bfloat16 [16384, 4096], P('dp', 'tensor'), may hold values from -6 to 6
- grad_out: bfloat16 [16384, 4608], P('dp', 'tensor'), may hold values from -6 to 6
- w_out: bfloat16 [4608, 4096], P('dp', 'tensor'), may hold values from -0.09375 to 0.09375
Outputs:
- d_attn: bfloat16 [16384, 4096], P('dp', 'tensor')
- o_grad: float32 [4608, 4096], P('dp', 'tensor')
Inputs may be any that keep to these rules, and one draw needn't show every extreme that they name: `pairs`: the two numbers of a pair differ. Each row of owner names every number once.
All inputs are finite; a program needn't handle non-finite values.
Results may differ from a plain program's by a relative error of at most 0.0049.
Values may be sent and summed in bfloat16 or wider, within the bound.
A program may use at most 128 MiB of HBM per device.

v0:
```python
import jax
import jax.numpy as jnp
from jax import lax
from jax.sharding import PartitionSpec as P

eta_scale = 2.0


def shards(
    embeds, owner, pairs, pref_weight, pref_bias, pref_out, logratio, attn_out, grad_out, w_out
):
    resp_dev = embeds.shape[0]
    prompts_dev = owner.shape[0]
    groups = owner.shape[1]
    npairs = pairs.shape[1]
    width_local = pref_weight.shape[2]
    features = lax.all_gather(grad_out, "tensor", axis=1, tiled=True)
    base = (jnp.arange(prompts_dev, dtype=jnp.int32) * groups)[:, None]
    row_a = base + jnp.take_along_axis(owner, pairs[:, :, 0], axis=1)
    row_b = base + jnp.take_along_axis(owner, pairs[:, :, 1], axis=1)
    left = embeds[row_a.reshape(-1)]
    right = embeds[row_b.reshape(-1)]
    piece = lax.all_gather(pref_weight, "dp", axis=1, tiled=True)
    upper = jnp.dot(left, piece[0], preferred_element_type=jnp.float32)
    lower = jnp.dot(right, piece[1], preferred_element_type=jnp.float32)
    pre = (upper + lower).reshape(prompts_dev, npairs, width_local)
    hidden = jax.nn.gelu(pre + pref_bias)
    partial_logit = jnp.sum(hidden * pref_out, axis=-1)
    logit = lax.psum(partial_logit, "tensor")
    prob = jax.nn.sigmoid(logit)
    numbers = jnp.arange(groups, dtype=jnp.int32)
    first = (pairs[:, :, 0][:, :, None] == numbers).astype(jnp.float32)
    second = (pairs[:, :, 1][:, :, None] == numbers).astype(jnp.float32)
    wins = jnp.sum(prob[:, :, None] * first + (1.0 - prob)[:, :, None] * second, axis=1)
    count = jnp.sum(first + second, axis=1)
    winrate = (wins + 1.0) / (count + 2.0)
    placed = (owner[:, :, None] == numbers).astype(jnp.float32)
    rowrate = jnp.sum(winrate[:, :, None] * placed, axis=1).reshape(-1)
    coef = 2.0 * (logratio - eta_scale * (rowrate - 0.5))
    weighted = (
        (
            features.astype(jnp.float32).reshape(resp_dev, -1, features.shape[1])
            * coef[:, None, None]
        )
        .reshape(features.shape)
        .astype(jnp.bfloat16)
    )
    piece = lax.all_gather(w_out, "dp", axis=0, tiled=True)
    block = weighted
    d_attn = jnp.dot(block, piece, preferred_element_type=jnp.float32).astype(jnp.bfloat16)
    total_resp = resp_dev * lax.axis_size("dp")
    block = weighted
    o_grad = (
        lax.psum_scatter(
            lax.dot_general(
                block, attn_out, (((0,), (0,)), ((), ())), preferred_element_type=jnp.float32
            ),
            "dp",
            scatter_dimension=0,
            tiled=True,
        )
        / total_resp
    )
    return (d_attn, o_grad)


def solution(mesh):
    return jax.shard_map(
        shards,
        mesh=mesh,
        in_specs=(
            P("dp", None),
            P("dp", None),
            P("dp", None, None),
            P(None, "dp", "tensor"),
            P("tensor"),
            P("tensor"),
            P("dp"),
            P("dp", "tensor"),
            P("dp", "tensor"),
            P("dp", "tensor"),
        ),
        out_specs=(P("dp", "tensor"), P("dp", "tensor")),
        check_vma=False,
    )
```

profile of v0, /device:TPU:0, one launch (start us, length us, event | category | flops | bytes accessed | tf_op | source)
XLA Modules:
  0.0 1243.1 jit_solution(2724786869625347840)
XLA Ops:
  7.2 0.7 all-gather.6.cloned.1.call-update
  8.0 0.7 all-gather.4.cloned.1.call-update
  8.7 0.7 all-gather.8.cloned.1.call-update
  9.5 0.8 fusion.20
  10.2 0.1 reshape.143
  10.3 2.2 gather_fusion.2
  12.5 0.1 reshape.146
  12.6 0.1 reshape.148
  12.7 2.0 gather_fusion.3
  14.7 0.1 reshape.151
  14.9 0.1 reshape.102
  15.1 1.2 gather_fusion.1
  16.3 1.2 gather_fusion
  17.5 431.0 %all-gather.6.cloned.1.call-done = bf16[2,4608,2304]{2,1,0:T(8,128)(2,1)} async-done(((bf16[2,288,2304]{2,1,0:T(8,128)(2,1)}), bf16[2,4608,2304]{2,1,0:T(8,128)(2,1)}) %all-gather.6.cloned.1.call-update) | async-done | bytes 42467344 | tf_op jit(solution)/shard_map/all_gather | solution.py:23
  448.5 9.8 fusion
  458.3 12.0 fusion.15
  470.4 2.6 psum.7
  473.1 0.1 add_reduce_fusion.1
  473.2 0.1 select_reduce_fusion
  473.5 28.3 %fusion.2 = f32[4608,2048]{1,0:T(8,128)} fusion(bf16[1024,2048]{1,0:T(8,128)(2,1)} %param.19, bf16[1024,4608]{1,0:T(8,128)(2,1)} %all-gather.4.cloned.1.call-done, f32[1024]{0:T(1024)S(1)} %mul.109), kind=kOutput, calls=%fused_computation.9 | convolution fusion | flops 19341508608 | bytes 51384320 | tf_op jit(solution)/shard_map/dot_general | solution.py:55
  501.9 183.7 %all-gather.8.cloned.1.call-done = bf16[4608,2048]{1,0:T(8,128)(2,1)} async-done(((bf16[288,2048]{1,0:T(8,128)(2,1)}), bf16[4608,2048]{1,0:T(8,128)(2,1)}) %all-gather.8.cloned.1.call-update) | async-done | bytes 18874384 | tf_op jit(solution)/shard_map/all_gather | solution.py:48
  685.6 26.5 %fusion.4 = bf16[1024,2048]{1,0:T(8,128)(2,1)} fusion(bf16[4608,2048]{1,0:T(8,128)(2,1)} %all-gather.8.cloned.1.call-done, bf16[1024,4608]{1,0:T(8,128)(2,1)} %all-gather.4.cloned.1.call-done, f32[1024]{0:T(1024)S(1)} %mul.109), kind=kOutput, calls=%fused_computation.11 | convolution fusion | flops 19343605760 | bytes 32509952 | tf_op jit(solution)/shard_map/dot_general | solution.py:50
  712.1 521.2 %reduce-scatter.2.cloned.1.call-done = f32[288,2048]{1,0:T(8,128)} async-done(((f32[4608,2048]{1,0:T(8,128)}), f32[288,2048]{1,0:T(8,128)}) %reduce-scatter.2.cloned.1.call-update) | async-done | bytes 2359312 | tf_op jit(solution)/shard_map/reduce_scatter | solution.py:54
  1233.3 3.3 broadcast_multiply_fusion
  (35 shorter events, 0.7 us)
Async XLA Ops:
  7.2 7.9 copy-start
  7.2 5.5 copy-start.2
  7.2 441.3 %all-gather.6.cloned.1.call-start = ((), (), s32[]{:S(2)}) async-start(), calls=%async_computation.2 | async-start | bytes 45121536 | tf_op jit(solution)/shard_map/all_gather | solution.py:23
  7.9 465.6 %all-gather.4.cloned.1.call-start = ((), (), s32[]{:S(2)}) async-start(), calls=%async_computation.1 | async-start | bytes 14155776 | tf_op jit(solution)/shard_map/all_gather | solution.py:17
  8.7 676.9 %all-gather.8.cloned.1.call-start = ((), (), s32[]{:S(2)}) async-start(), calls=%async_computation.3 | async-start | bytes 20054016 | tf_op jit(solution)/shard_map/all_gather | solution.py:48
  9.4 1223.8 %reduce-scatter.2.cloned.1.call-start = ((), (), s32[]{:S(2)}) async-start(), calls=%async_computation.4 | async-start | bytes 40108032 | tf_op jit(solution)/shard_map/reduce_scatter | solution.py:54
  17.4 440.9 %copy-start.3 = (f32[2304]{0:T(1024)S(1)}, f32[2304]{0:T(1024)}, u32[]{:S(2)}) copy-start(f32[2304]{0:T(1024)} %param.17) | copy-start | bytes 27652
  17.4 440.9 %copy-start.4 = (f32[2304]{0:T(1024)S(1)}, f32[2304]{0:T(1024)}, u32[]{:S(2)}) copy-start(f32[2304]{0:T(1024)} %param.16) | copy-start | bytes 27652
  458.3 15.0 %copy-start.5 = (f32[16]{0:T(128)S(1)}, f32[16]{0:T(128)}, u32[]{:S(2)}) copy-start(f32[16]{0:T(128)} %param.18) | copy-start | bytes 196
  685.6 551.0 %copy-start.1 = (bf16[16,4608]{1,0:T(8,128)(2,1)S(1)}, bf16[16,4608]{1,0:T(8,128)(2,1)}, u32[]{:S(2)}) copy-start(bf16[16,4608]{1,0:T(8,128)(2,1)} %param.12) | copy-start | bytes 442372
Sparse Core Ops, SparseCore 0:
  10.7 437.7 all-gather.5
  450.1 19.9 all-gather.3
  472.9 212.6 all-gather.7
  691.5 541.7 reduce-scatter.1
where the time goes:
time: 1240 us
  waiting for transfers between devices  1140 us (92%)
  matrix products  76.6 us (6%)
  between operations  13.9 us (1%)
    reduce_scatter x1, waiting for transfers between devices, shards(): lax.psum_scatter(lax.dot_general(block, attn_out, (((0,), (0,)), ((), ())...  521 us
    all_gather x1, waiting for transfers between devices, shards(): piece = lax.all_gather(pref_weight, 'dp', axis=1, tiled=True)  431 us
    all_gather x1, waiting for transfers between devices, shards(): piece = lax.all_gather(w_out, 'dp', axis=0, tiled=True)  184 us
    dot_general x1, matrix products, shards(): lax.dot_general(block, attn_out, (((0,), (0,)), ((), ())), preferred_elem...  28.3 us
    dot_general x1, matrix products, shards(): jnp.dot(block, piece, preferred_element_type=jnp.float32)  26.5 us
  transfers between devices with their start and end apart: 4, of which 3 were waited for; matrix products, arithmetic and copies ran while one was open for 7% of the time, Pallas kernels for 0%

commit v1 on v0

v1 whole, which is shorter than its diff:
```python
import jax
import jax.numpy as jnp
from jax import lax
from jax.sharding import PartitionSpec as P

eta_scale = 2.0
NX = 2
NY = 2
CHUNKS = 4


def x_pairs(n):
    return [(i, i ^ 1) for i in range(n)]


def y_pairs(n):
    return [(i, i ^ NX) for i in range(n)]


def z_pairs(n, step, sign, outward):
    plane = NX * NY
    nz = n // plane
    pairs = []
    for i in range(n):
        k = i // plane
        far = k if sign > 0 else nz - 1 - k
        if far == nz - 1:
            continue
        if (far >= step - 1) if outward else (far <= step - 1):
            pairs.append((i, i + sign * plane))
    return pairs


def at(array, index):
    return lax.dynamic_index_in_dim(array, index, 0, keepdims=False)


def line_reduce(own, z, n, dtype):
    nz = own.shape[0]
    right = left = None
    for step in range(1, nz):
        give_r = at(own, jnp.clip(nz - step + z, 0, nz - 1))
        give_l = at(own, jnp.clip(z - nz + step, 0, nz - 1))
        if right is not None:
            give_r = give_r + right.astype(jnp.float32)
            give_l = give_l + left.astype(jnp.float32)
        right = lax.ppermute(give_r.astype(dtype), "dp", z_pairs(n, step, 1, False))
        left = lax.ppermute(give_l.astype(dtype), "dp", z_pairs(n, step, -1, False))
    return at(own, z) + right.astype(jnp.float32) + left.astype(jnp.float32)


def line_gather(own, z, n):
    nz = n // (NX * NY)
    rights, lefts = [], []
    right = left = own
    for step in range(1, nz):
        right = lax.ppermute(right, "dp", z_pairs(n, step, 1, True))
        left = lax.ppermute(left, "dp", z_pairs(n, step, -1, True))
        rights.append(right)
        lefts.append(left)
    line = jnp.stack(rights[::-1] + [own] + lefts)
    return lax.dynamic_slice_in_dim(line, nz - 1 - z, nz, 0)


def in_order(first, own, other, axis):
    return jnp.where(
        first,
        jnp.concatenate([own, other], axis=axis),
        jnp.concatenate([other, own], axis=axis),
    )


def shards(
    embeds, owner, pairs, pref_weight, pref_bias, pref_out, logratio, attn_out, grad_out, w_out
):
    n = lax.axis_size("dp")
    nz = n // (NX * NY)
    me = lax.axis_index("dp")
    x, y, z = me % NX, (me // NX) % NY, me // (NX * NY)
    resp_dev, width = embeds.shape
    prompts_dev, groups = owner.shape
    npairs = pairs.shape[1]
    part, hidden_local = pref_weight.shape[1:]
    tokens = grad_out.shape[0]
    half = attn_out.shape[1] // NX
    rows_out = w_out.shape[0]

    grad_other = lax.ppermute(grad_out, "dp", x_pairs(n))
    features = lax.all_gather(grad_out, "tensor", axis=1, tiled=True)
    features_other = lax.all_gather(grad_other, "tensor", axis=1, tiled=True)
    attn_mine = lax.dynamic_slice_in_dim(attn_out, x * half, half, 1)
    attn_send = lax.dynamic_slice_in_dim(attn_out, (1 - x) * half, half, 1)
    attn_other = lax.ppermute(attn_send, "dp", x_pairs(n))
    attn_both = jnp.concatenate([attn_mine, attn_other], axis=0)

    cut = embeds.reshape(resp_dev, n, part).transpose(1, 0, 2)
    cut = lax.all_to_all(cut, "dp", 0, 0, tiled=True).reshape(n * resp_dev, part)
    partial = jnp.stack(
        [
            jnp.dot(cut, pref_weight[s], preferred_element_type=jnp.float32)
            for s in range(2)
        ],
        axis=1,
    ).reshape(nz, NY, NX, resp_dev, 2, hidden_local)
    keep = lax.dynamic_index_in_dim(partial, y, 1, keepdims=False)
    send = lax.dynamic_index_in_dim(partial, 1 - y, 1, keepdims=False)
    keep = keep + lax.ppermute(send, "dp", y_pairs(n))
    keep = line_reduce(keep, z, n, jnp.float32)
    both = at(keep, x) + lax.ppermute(at(keep, 1 - x), "dp", x_pairs(n))
    upper, lower = both[:, 0], both[:, 1]

    base = (jnp.arange(prompts_dev, dtype=jnp.int32) * groups)[:, None]
    row_a = base + jnp.take_along_axis(owner, pairs[:, :, 0], axis=1)
    row_b = base + jnp.take_along_axis(owner, pairs[:, :, 1], axis=1)
    pre = upper[row_a.reshape(-1)] + lower[row_b.reshape(-1)]
    pre = pre.reshape(prompts_dev, npairs, hidden_local)
    hidden = jax.nn.gelu(pre + pref_bias)
    logit = lax.psum(jnp.sum(hidden * pref_out, axis=-1), "tensor")
    prob = jax.nn.sigmoid(logit)
    numbers = jnp.arange(groups, dtype=jnp.int32)
    first = (pairs[:, :, 0][:, :, None] == numbers).astype(jnp.float32)
    second = (pairs[:, :, 1][:, :, None] == numbers).astype(jnp.float32)
    wins = jnp.sum(prob[:, :, None] * first + (1.0 - prob)[:, :, None] * second, axis=1)
    count = jnp.sum(first + second, axis=1)
    winrate = (wins + 1.0) / (count + 2.0)
    placed = (owner[:, :, None] == numbers).astype(jnp.float32)
    rowrate = jnp.sum(winrate[:, :, None] * placed, axis=1).reshape(-1)
    coef = 2.0 * (logratio - eta_scale * (rowrate - 0.5))
    coef_other = lax.ppermute(coef, "dp", x_pairs(n))

    def scale(block, by):
        shaped = block.astype(jnp.float32).reshape(resp_dev, -1, width)
        return (shaped * by[:, None, None]).reshape(block.shape).astype(jnp.bfloat16)

    weighted = jnp.concatenate([scale(features, coef), scale(features_other, coef_other)], axis=0)

    w_other = lax.ppermute(
        lax.dynamic_slice_in_dim(w_out, (1 - x) * half, half, 1), "dp", x_pairs(n)
    )
    w_mine = lax.dynamic_slice_in_dim(w_out, x * half, half, 1)
    w_pair = in_order(x == 0, w_mine, w_other, 0)
    w_line = line_gather(w_pair, z, n)
    w_line_other = lax.ppermute(w_line, "dp", y_pairs(n))
    w_all = in_order(y == 0, w_line[:, None], w_line_other[:, None], 1).reshape(-1, half)

    step = half // CHUNKS
    pieces = []
    for c in range(CHUNKS):
        block = lax.dot_general(
            weighted,
            attn_both[:, c * step : (c + 1) * step],
            (((0,), (0,)), ((), ())),
            preferred_element_type=jnp.float32,
        ).reshape(nz, NY, NX * rows_out, step)
        mine = lax.dynamic_index_in_dim(block, y, 1, keepdims=False)
        away = lax.dynamic_index_in_dim(block, 1 - y, 1, keepdims=False).astype(jnp.bfloat16)
        mine = mine + lax.ppermute(away, "dp", y_pairs(n)).astype(jnp.float32)
        pieces.append(line_reduce(mine, z, n, jnp.bfloat16))

    d_send = jnp.dot(weighted[tokens:], w_all, preferred_element_type=jnp.float32).astype(
        jnp.bfloat16
    )
    d_other = lax.ppermute(d_send, "dp", x_pairs(n))
    d_mine = jnp.dot(weighted[:tokens], w_all, preferred_element_type=jnp.float32).astype(
        jnp.bfloat16
    )
    d_attn = in_order(x == 0, d_mine, d_other, 1)

    total_resp = resp_dev * n
    summed = jnp.concatenate(pieces, axis=1).reshape(NX, rows_out, half)
    o_other = lax.ppermute(at(summed, 1 - x).astype(jnp.bfloat16), "dp", x_pairs(n))
    o_grad = in_order(x == 0, at(summed, x), o_other.astype(jnp.float32), 1) / total_resp
    return (d_attn, o_grad)


def solution(mesh):
    return jax.shard_map(
        shards,
        mesh=mesh,
        in_specs=(
            P("dp", None),
            P("dp", None),
            P("dp", None, None),
            P(None, "dp", "tensor"),
            P("tensor"),
            P("tensor"),
            P("dp"),
            P("dp", "tensor"),
            P("dp", "tensor"),
            P("dp", "tensor"),
        ),
        out_specs=(P("dp", "tensor"), P("dp", "tensor")),
        check_vma=False,
    )
```

time: 1240 us -> 567 us (0.46); the launches traced: 1240 us -> 557 us
  waiting for transfers between devices: 1140 us -> 198 us
  starting transfers between devices: 0.15 us -> 132 us
  other arithmetic: 3.66 us -> 66.4 us
  local copies, waits for them, and re-layouts: 8.16 us -> 68.3 us
    all_gather x2 -> x1, waiting for transfers between devices: 615 us -> 0.01 us  [shards(): features_other = lax.all_gather(grad_other, 'tensor', axis=1, tiled=True)]
    reduce_scatter x1 -> x0, waiting for transfers between devices: 521 us -> none  [shards(): lax.psum_scatter(lax.dot_general(block, attn_out, (((0,), (0,)), ((), ())...]
    ppermute x0 -> x49, waiting for transfers between devices: none -> 189 us  [the longest x1 60.1 us: shards(): w_line_other = lax.ppermute(w_line, 'dp', y_pairs(n))]
    ppermute x0 -> x49, starting transfers between devices: none -> 124 us  [the longest x15 83.9 us: line_reduce(): right = lax.ppermute(give_r.astype(dtype), 'dp', z_pairs(n, step, 1, False))]
    convert_element_type x0 -> x15, other arithmetic: none -> 22.5 us  [the longest x2 21.1 us: scale(): (shaped * by[:, None, None]).reshape(block.shape).astype(jnp.bfloat16)]
    unnamed x12 -> x42, local copies, waits for them, and re-layouts: 0.04 us -> 22.5 us
    select_n x2 -> x5, other arithmetic: 0.01 us -> 18.9 us  [the longest x3 18.9 us: in_order(): jnp.where(first, jnp.concatenate([own, other], axis=axis), jnp.concatenat...]
    add x1 -> x15, other arithmetic: 0.07 us -> 17.9 us  [the longest x4 6.61 us: shards(): mine = mine + lax.ppermute(away, 'dp', y_pairs(n)).astype(jnp.float32)]
  transfers between devices with their start and end apart: 4 -> 52, of which waited for: 3 -> 20; matrix products, arithmetic and copies ran while one was open for 7% -> 36% of each run, Pallas kernels for 0% -> 0%
where the time goes in v1:
time: 567 us; the launch traced here: 557 us
  waiting for transfers between devices  198 us (35%)
  starting transfers between devices  132 us (23%)
  matrix products  74.2 us (13%)
  local copies, waits for them, and re-layouts  68.3 us (12%)
  other arithmetic  66.4 us (12%)
  between operations  15.3 us (3%)
    ppermute x15, starting transfers between devices, line_reduce(): right = lax.ppermute(give_r.astype(dtype), 'dp', z_pairs(n, step, 1, False))  83.9 us
    ppermute x1, waiting for transfers between devices, shards(): w_line_other = lax.ppermute(w_line, 'dp', y_pairs(n))  60.1 us
    dot_general x4, matrix products, shards(): lax.dot_general(weighted, attn_both[:, c * step:(c + 1) * step], (((0,),...  40 us
    ppermute x4, waiting for transfers between devices, shards(): mine = mine + lax.ppermute(away, 'dp', y_pairs(n)).astype(jnp.float32)  37.4 us
    ppermute x1, waiting for transfers between devices, shards(): keep = keep + lax.ppermute(send, 'dp', y_pairs(n))  25.1 us
    unnamed x42, local copies, waits for them, and re-layouts  22.5 us
    convert_element_type x2, other arithmetic, scale(): (shaped * by[:, None, None]).reshape(block.shape).astype(jnp.bfloat16)  21.1 us
    select_n x3, other arithmetic, in_order(): jnp.where(first, jnp.concatenate([own, other], axis=axis), jnp.concatenat...  18.9 us
  transfers between devices with their start and end apart: 52, of which 20 were waited for; matrix products, arithmetic and copies ran while one was open for 36% of the time, Pallas kernels for 0%

profile of v1, /device:TPU:0, one launch (start us, length us, event | category | flops | bytes accessed | tf_op | source)
XLA Modules:
  0.0 557.2 jit_solution(2687838837324438408)
XLA Ops:
  9.1 8.3 %all-to-all-start = ((bf16[16,16,288]{2,1,0:T(8,128)(2,1)}), bf16[16,16,288]{2,1,0:T(8,128)(2,1)S(1)}, u32[]{:S(2)}, u32[]{:S(2)}) async-start(bf16[16,16,288]{2,1,0:T(8,128)(2,1)} %bitcast.221), calls=%async_computation | async-start | bytes 393216 | tf_op jit(solution)/shard_map/all_to_all | solution.py:97
  17.5 8.5 %all-to-all-done = bf16[16,16,288]{2,1,0:T(8,128)(2,1)S(1)} async-done(((bf16[16,16,288]{2,1,0:T(8,128)(2,1)}), bf16[16,16,288]{2,1,0:T(8,128)(2,1)S(1)}, u32[]{:S(2)}, u32[]{:S(2)}) %all-to-all-start) | async-done | bytes 147488 | tf_op jit(solution)/shard_map/all_to_all | solution.py:97
  36.2 14.5 %collective-permute-done.8 = bf16[288,1024]{1,0:T(8,128)(2,1)S(1)} collective-permute-done((bf16[288,1024]{1,0:T(8,128)(2,1)}, bf16[288,1024]{1,0:T(8,128)(2,1)S(1)}, u32[]{:S(2)}, u32[]{:S(2)}) %collective-permute-start.8) | collective-permute-done | bytes 589856 | tf_op jit(solution)/shard_map/ppermute | solution.py:137
  57.3 25.1 %collective-permute-done = f32[4,2,16,2,2304]{4,2,3,1,0:T(8,128)S(1)} collective-permute-done((f32[4,2,16,2,2304]{4,2,3,1,0:T(8,128)}, f32[4,2,16,2,2304]{4,2,3,1,0:T(8,128)S(1)}, u32[]{:S(2)}, u32[]{:S(2)}) %collective-permute-start) | collective-permute-done | bytes 2359328 | tf_op jit(solution)/shard_map/ppermute | solution.py:107
  132.8 7.3 %collective-permute-start.3 = (f32[2,16,2,2304]{3,1,2,0:T(8,128)}, f32[2,16,2,2304]{3,1,2,0:T(8,128)}, u32[]{:S(2)}, u32[]{:S(2)}) collective-permute-start(f32[2,16,2,2304]{3,1,2,0:T(8,128)} %get-tuple-element.35), channel_id=1, source_target_pairs={{0,8},{2,10},{4,12},{6,14},{8,16},{10,18},{12,20},{14,22},{16,24},... | collective-permute-start | bytes 1769480 | tf_op jit(solution)/shard_map/ppermute | solution.py:47
  144.9 7.0 %collective-permute-done.16 = bf16[1024,2304]{1,0:T(8,128)(2,1)} collective-permute-done((bf16[1024,2304]{1,0:T(8,128)(2,1)}, bf16[1024,2304]{1,0:T(8,128)(2,1)}, u32[]{:S(2)}, u32[]{:S(2)}) %collective-permute-start.16) | collective-permute-done | bytes 4718624 | tf_op jit(solution)/shard_map/ppermute | solution.py:88
  166.1 6.5 %constant_dynamic-slice_fusion.2 = bf16[4,576,1024]{2,1,0:T(8,128)(2,1)} fusion(bf16[7,576,1024]{2,1,0:T(8,128)(2,1)} %bitcast_dynamic-update-slice_fusion, s32[]{:T(128)S(6)} %select_n.186), kind=kLoop, calls=%fused_computation.148 | loop fusion | bytes 9437188 | tf_op jit(solution)/shard_map/dynamic_slice | solution.py:62
  183.9 15.7 %collective-permute-done.7 = f32[16,2,2304]{2,0,1:T(8,128)S(1)} collective-permute-done((f32[16,2,2304]{2,0,1:T(8,128)S(1)}, f32[16,2,2304]{2,0,1:T(8,128)S(1)}, u32[]{:S(2)}, u32[]{:S(2)}) %collective-permute-start.7) | collective-permute-done | bytes 294944 | tf_op jit(solution)/shard_map/ppermute | solution.py:109
  209.1 60.1 %collective-permute-done.15 = bf16[4,576,1024]{2,1,0:T(8,128)(2,1)} collective-permute-done((bf16[4,576,1024]{2,1,0:T(8,128)(2,1)}, bf16[4,576,1024]{2,1,0:T(8,128)(2,1)}, u32[]{:S(2)}, u32[]{:S(2)}) %collective-permute-start.15) | collective-permute-done | bytes 4718624 | tf_op jit(solution)/shard_map/ppermute | solution.py:143
  269.2 11.7 %maximum_select_fusion = bf16[4,2,576,1024]{3,2,1,0:T(8,128)(2,1)} fusion(bf16[4,1,576,1024]{3,2,1,0:T(8,128)(2,1)} %bitcast.38, bf16[4,1,576,1024]{3,2,1,0:T(8,128)(2,1)} %fusion.77, pred[]{:T(512)S(6)} %eq.63), kind=kLoop, calls=%fused_computation.7 | loop fusion | flops 14155776 | bytes 18874368 | tf_op jit(solution)/shard_map/jit(_where)/select_n | solution.py:66
  280.9 10.5 %multiply_convert_fusion.1 = bf16[1024,4608]{1,0:T(8,128)(2,1)} fusion(bf16[1024,4608]{1,0:T(8,128)(2,1)} %all-gather.3.cloned.1.call-done, f32[1024]{0:T(1024)S(1)} %mul.130), kind=kLoop, calls=%fused_computation.6 | loop fusion | flops 14155776 | bytes 18878464 | tf_op jit(solution)/shard_map/convert_element_type | solution.py:133
  291.4 10.5 %multiply_convert_fusion = bf16[1024,4608]{1,0:T(8,128)(2,1)} fusion(bf16[1024,4608]{1,0:T(8,128)(2,1)} %all-gather.5.cloned.1.call-done, f32[1024]{0:T(1024)S(1)} %mul.136), kind=kLoop, calls=%fused_computation.5 | loop fusion | flops 14155776 | bytes 18878464 | tf_op jit(solution)/shard_map/convert_element_type | solution.py:133
  302.0 16.4 %convolution_convert_fusion = bf16[1024,1024]{0,1:T(8,128)(2,1)} fusion(bf16[1024,4608]{1,0:T(8,128)(2,1)} %multiply_convert_fusion, bf16[4608,1024]{1,0:T(8,128)(2,1)} %bitcast.224), kind=kOutput, calls=%fused_computation.36 | convolution fusion | flops 9664724992 | bytes 20971520 | tf_op jit(solution)/shard_map/dot_general | solution.py:160
  319.9 9.9 %fusion.21 = f32[4608,256]{1,0:T(8,128)S(1)} fusion(bf16[1024,1024]{1,0:T(8,128)(2,1)} %collective-permute-done.19, bf16[1024,1024]{1,0:T(8,128)(2,1)S(1)} %copy-done.3, bf16[1024,4608]{1,0:T(8,128)(2,1)} %multiply_convert_fusion, bf16[1024,4608]{1,0:T(8,128)(2,1)} %multiply_convert_fusion.1), kind=kOutput, calls=%fused_computation.65 | convolution fusion | flops 4871684096 | bytes 27787264 | tf_op jit(solution)/shard_map/dot_general | solution.py:149
  334.9 11.1 %fusion.13 = f32[4608,256]{1,0:T(8,128)} fusion(bf16[1024,1024]{1,0:T(8,128)(2,1)} %get-tuple-element.17, bf16[1024,1024]{1,0:T(8,128)(2,1)} %collective-permute-done.19, bf16[1024,4608]{1,0:T(8,128)(2,1)} %multiply_convert_fusion, bf16[1024,4608]{1,0:T(8,128)(2,1)} %multiply_convert_fusion.1), kind=kOutput, calls=%fused_computation.59 | convolution fusion | flops 4871684096 | bytes 27787264 | tf_op jit(solution)/shard_map/dot_general | solution.py:149
  349.5 9.5 %fusion.19 = f32[4608,256]{1,0:T(8,128)} fusion(bf16[1024,1024]{1,0:T(8,128)(2,1)} %get-tuple-element.17, bf16[1024,1024]{1,0:T(8,128)(2,1)} %collective-permute-done.19, bf16[1024,4608]{1,0:T(8,128)(2,1)} %multiply_convert_fusion, bf16[1024,4608]{1,0:T(8,128)(2,1)S(1)} %bitcast.223), kind=kOutput, calls=%fused_computation.63 | convolution fusion | flops 4871684096 | bytes 27787264 | tf_op jit(solution)/shard_map/dot_general | solution.py:149
  362.2 9.5 %fusion.16 = f32[4608,256]{1,0:T(8,128)} fusion(bf16[1024,1024]{1,0:T(8,128)(2,1)} %get-tuple-element.17, bf16[1024,1024]{1,0:T(8,128)(2,1)} %collective-permute-done.19, bf16[1024,4608]{1,0:T(8,128)(2,1)} %multiply_convert_fusion, bf16[1024,4608]{1,0:T(8,128)(2,1)S(1)} %bitcast.223), kind=kOutput, calls=%fused_computation.61 | convolution fusion | flops 4871684096 | bytes 27787264 | tf_op jit(solution)/shard_map/dot_general | solution.py:149
  390.8 22.1 %collective-permute-done.27 = bf16[4,576,256]{2,1,0:T(8,128)(2,1)} collective-permute-done((bf16[4,576,256]{2,1,0:T(8,128)(2,1)S(1)}, bf16[4,576,256]{2,1,0:T(8,128)(2,1)}, u32[]{:S(2)}, u32[]{:S(2)}) %collective-permute-start.27) | collective-permute-done | bytes 1179680 | tf_op jit(solution)/shard_map/ppermute | solution.py:157
  412.9 5.6 %collective-permute-start.35 = (bf16[576,256]{1,0:T(8,128)(2,1)S(1)}, bf16[576,256]{1,0:T(8,128)(2,1)S(1)}, u32[]{:S(2)}, u32[]{:S(2)}) collective-permute-start(bf16[576,256]{1,0:T(8,128)(2,1)S(1)} %get-tuple-element.29), channel_id=1, source_target_pairs={{0,8},{2,10},{4,12},{6,14},{1,9},{3,11},{5,13},{7,15}} | collective-permute-start | bytes 884744 | tf_op jit(solution)/shard_map/ppermute | solution.py:47
  420.2 10.3 %collective-permute-done.20 = bf16[4,576,256]{2,1,0:T(8,128)(2,1)S(1)} collective-permute-done((bf16[4,576,256]{2,1,0:T(8,128)(2,1)S(1)}, bf16[4,576,256]{2,1,0:T(8,128)(2,1)S(1)}, u32[]{:S(2)}, u32[]{:S(2)}) %collective-permute-start.20) | collective-permute-done | bytes 1179680 | tf_op jit(solution)/shard_map/ppermute | solution.py:157
  438.4 5.9 %collective-permute-done.28 = bf16[576,256]{1,0:T(8,128)(2,1)S(1)} collective-permute-done((bf16[576,256]{1,0:T(8,128)(2,1)S(1)}, bf16[576,256]{1,0:T(8,128)(2,1)S(1)}, u32[]{:S(2)}, u32[]{:S(2)}) %collective-permute-start.28) | collective-permute-done | bytes 294944 | tf_op jit(solution)/shard_map/ppermute | solution.py:47
  483.8 18.8 %collective-permute-start.30 = (bf16[576,256]{1,0:T(8,128)(2,1)S(1)}, bf16[576,256]{1,0:T(8,128)(2,1)S(1)}, u32[]{:S(2)}, u32[]{:S(2)}) collective-permute-start(bf16[576,256]{1,0:T(8,128)(2,1)S(1)} %get-tuple-element.23), channel_id=1, source_target_pairs={{0,8},{2,10},{4,12},{6,14},{8,16},{10,18},{12,20},{14,22},{16,24},... | collective-permute-start | bytes 884744 | tf_op jit(solution)/shard_map/ppermute | solution.py:47
  519.5 16.2 %convolution_convert_fusion.1 = bf16[1024,1024]{0,1:T(8,128)(2,1)} fusion(bf16[1024,4608]{1,0:T(8,128)(2,1)} %multiply_convert_fusion.1, bf16[4608,1024]{1,0:T(8,128)(2,1)} %bitcast.225), kind=kOutput, calls=%fused_computation.37 | convolution fusion | flops 9664724992 | bytes 20971520 | tf_op jit(solution)/shard_map/dot_general | solution.py:164
  541.4 6.4 %copy.39 = bf16[1024,2048]{1,0:T(8,128)(2,1)} copy(bf16[1024,2048]{0,1:T(8,128)(2,1)} %maximum_select_fusion.1) | data formatting | bytes 8388608
  (224 shorter events, 214.3 us)
Async XLA Ops:
  7.2 273.7 %all-gather.3.cloned.1.call-start = ((), (), s32[]{:S(2)}) async-start(), calls=%async_computation.1 | async-start | bytes 14155776 | tf_op jit(solution)/shard_map/all_gather | solution.py:89
  17.4 274.0 %all-gather.5.cloned.1.call-start = ((), (), s32[]{:S(2)}) async-start(), calls=%async_computation.2 | async-start | bytes 14155776 | tf_op jit(solution)/shard_map/all_gather | solution.py:90
  31.0 51.4 %collective-permute-start = (f32[4,2,16,2,2304]{4,2,3,1,0:T(8,128)}, f32[4,2,16,2,2304]{4,2,3,1,0:T(8,128)S(1)}, u32[]{:S(2)}, u32[]{:S(2)}) collective-permute-start(f32[4,2,16,2,2304]{4,2,3,1,0:T(8,128)} %bitcast.220), channel_id=1, source_target_pairs={{0,4},{2,6},{4,0},{6,2},{8,12},{10,14},{12,8},{14,10},{16,20},{18,... | collective-permute-start | bytes 7077896 | tf_op jit(solution)/shard_map/ppermute | solution.py:107
  34.7 117.2 %collective-permute-start.16 = (bf16[1024,2304]{1,0:T(8,128)(2,1)}, bf16[1024,2304]{1,0:T(8,128)(2,1)}, u32[]{:S(2)}, u32[]{:S(2)}) collective-permute-start(bf16[1024,2304]{1,0:T(8,128)(2,1)} %param.20), channel_id=1, source_target_pairs={{0,2},{2,0},{4,6},{6,4},{8,10},{10,8},{12,14},{14,12},{16,18},{18,... | collective-permute-start | bytes 14155784 | tf_op jit(solution)/shard_map/ppermute | solution.py:88
  52.2 38.8 %collective-permute-start.9 = (bf16[576,1024]{1,0:T(8,128)(2,1)}, bf16[576,1024]{1,0:T(8,128)(2,1)}, u32[]{:S(2)}, u32[]{:S(2)}) collective-permute-start(bf16[576,1024]{1,0:T(8,128)(2,1)} %maximum_select_fusion.3), channel_id=1, source_target_pairs={{0,8},{2,10},{4,12},{6,14},{8,16},{10,18},{12,20},{14,22},{16,24},... | collective-permute-start | bytes 3538952 | tf_op jit(solution)/shard_map/ppermute | solution.py:57
  56.0 36.8 %collective-permute-start.12 = (bf16[576,1024]{1,0:T(8,128)(2,1)}, bf16[576,1024]{1,0:T(8,128)(2,1)}, u32[]{:S(2)}, u32[]{:S(2)}) collective-permute-start(bf16[576,1024]{1,0:T(8,128)(2,1)} %maximum_select_fusion.3), channel_id=1, source_target_pairs={{8,0},{10,2},{12,4},{14,6},{16,8},{18,10},{20,12},{22,14},{24,16},... | collective-permute-start | bytes 3538952 | tf_op jit(solution)/shard_map/ppermute | solution.py:58
  92.8 33.4 %collective-permute-start.13 = (bf16[576,1024]{1,0:T(8,128)(2,1)}, bf16[576,1024]{1,0:T(8,128)(2,1)}, u32[]{:S(2)}, u32[]{:S(2)}) collective-permute-start(bf16[576,1024]{1,0:T(8,128)(2,1)} %collective-permute-done.12), channel_id=1, source_target_pairs={{8,0},{10,2},{12,4},{14,6},{16,8},{18,10},{20,12},{22,14},{9,1},{1... | collective-permute-start | bytes 3538952 | tf_op jit(solution)/shard_map/ppermute | solution.py:58
  94.1 33.5 %collective-permute-start.4 = (f32[2,16,2,2304]{3,1,2,0:T(8,128)}, f32[2,16,2,2304]{3,1,2,0:T(8,128)}, u32[]{:S(2)}, u32[]{:S(2)}) collective-permute-start(f32[2,16,2,2304]{3,1,2,0:T(8,128)} %get-tuple-element.38), channel_id=1, source_target_pairs={{24,16},{26,18},{28,20},{30,22},{25,17},{27,19},{29,21},{31,23}} | collective-permute-start | bytes 1769480 | tf_op jit(solution)/shard_map/ppermute | solution.py:48
  102.2 26.7 %collective-permute-start.2 = (f32[2,16,2,2304]{3,1,2,0:T(8,128)}, f32[2,16,2,2304]{3,1,2,0:T(8,128)}, u32[]{:S(2)}, u32[]{:S(2)}) collective-permute-start(f32[2,16,2,2304]{3,1,2,0:T(8,128)} %bitcast_add_fusion.27), channel_id=1, source_target_pairs={{0,8},{2,10},{4,12},{6,14},{8,16},{10,18},{12,20},{14,22},{1,9},{3... | collective-permute-start | bytes 1769480 | tf_op jit(solution)/shard_map/ppermute | solution.py:47
  126.1 193.8 %collective-permute-start.19 = (bf16[1024,1024]{1,0:T(8,128)(2,1)}, bf16[1024,1024]{1,0:T(8,128)(2,1)}, u32[]{:S(2)}, u32[]{:S(2)}) collective-permute-start(bf16[1024,1024]{1,0:T(8,128)(2,1)} %get-tuple-element.18), channel_id=1, source_target_pairs={{0,2},{2,0},{4,6},{6,4},{8,10},{10,8},{12,14},{14,12},{16,18},{18,... | collective-permute-start | bytes 6291464 | tf_op jit(solution)/shard_map/ppermute | solution.py:93
  127.5 33.4 %collective-permute-start.14 = (bf16[576,1024]{1,0:T(8,128)(2,1)}, bf16[576,1024]{1,0:T(8,128)(2,1)}, u32[]{:S(2)}, u32[]{:S(2)}) collective-permute-start(bf16[576,1024]{1,0:T(8,128)(2,1)} %collective-permute-done.13), channel_id=1, source_target_pairs={{8,0},{10,2},{12,4},{14,6},{9,1},{11,3},{13,5},{15,7}} | collective-permute-start | bytes 3538952 | tf_op jit(solution)/shard_map/ppermute | solution.py:58
  131.3 32.2 %collective-permute-start.5 = (f32[2,16,2,2304]{3,1,2,0:T(8,128)}, f32[2,16,2,2304]{3,1,2,0:T(8,128)}, u32[]{:S(2)}, u32[]{:S(2)}) collective-permute-start(f32[2,16,2,2304]{3,1,2,0:T(8,128)} %get-tuple-element.36), channel_id=1, source_target_pairs={{16,8},{18,10},{20,12},{22,14},{24,16},{26,18},{28,20},{30,22},{17... | collective-permute-start | bytes 1769480 | tf_op jit(solution)/shard_map/ppermute | solution.py:48
  132.8 40.2 %collective-permute-start.3 = (f32[2,16,2,2304]{3,1,2,0:T(8,128)}, f32[2,16,2,2304]{3,1,2,0:T(8,128)}, u32[]{:S(2)}, u32[]{:S(2)}) collective-permute-start(f32[2,16,2,2304]{3,1,2,0:T(8,128)} %get-tuple-element.35), channel_id=1, source_target_pairs={{0,8},{2,10},{4,12},{6,14},{8,16},{10,18},{12,20},{14,22},{16,24},... | collective-permute-start | bytes 1769480 | tf_op jit(solution)/shard_map/ppermute | solution.py:47
  172.6 96.6 %collective-permute-start.15 = (bf16[4,576,1024]{2,1,0:T(8,128)(2,1)}, bf16[4,576,1024]{2,1,0:T(8,128)(2,1)}, u32[]{:S(2)}, u32[]{:S(2)}) collective-permute-start(bf16[4,576,1024]{2,1,0:T(8,128)(2,1)} %constant_dynamic-slice_fusion.2), channel_id=1, source_target_pairs={{0,4},{2,6},{4,0},{6,2},{8,12},{10,14},{12,8},{14,10},{16,20},{18,... | collective-permute-start | bytes 14155784 | tf_op jit(solution)/shard_map/ppermute | solution.py:143
  318.3 217.4 %collective-permute-start.18 = (bf16[1024,1024]{0,1:T(8,128)(2,1)}, bf16[1024,1024]{0,1:T(8,128)(2,1)}, u32[]{:S(2)}, u32[]{:S(2)}) collective-permute-start(bf16[1024,1024]{0,1:T(8,128)(2,1)} %convolution_convert_fusion), channel_id=1, source_target_pairs={{0,2},{2,0},{4,6},{6,4},{8,10},{10,8},{12,14},{14,12},{16,18},{18,... | collective-permute-start | bytes 6291464 | tf_op jit(solution)/shard_map/ppermute | solution.py:163
  333.1 41.3 %collective-permute-start.41 = (bf16[4,576,256]{2,1,0:T(8,128)(2,1)}, bf16[4,576,256]{2,1,0:T(8,128)(2,1)}, u32[]{:S(2)}, u32[]{:S(2)}) collective-permute-start(bf16[4,576,256]{2,1,0:T(8,128)(2,1)} %fusion.10), channel_id=1, source_target_pairs={{0,4},{2,6},{4,0},{6,2},{8,12},{10,14},{12,8},{14,10},{16,20},{18,... | collective-permute-start | bytes 3538952 | tf_op jit(solution)/shard_map/ppermute | solution.py:157
  348.8 38.8 %collective-permute-start.34 = (bf16[4,576,256]{2,1,0:T(8,128)(2,1)}, bf16[4,576,256]{2,1,0:T(8,128)(2,1)}, u32[]{:S(2)}, u32[]{:S(2)}) collective-permute-start(bf16[4,576,256]{2,1,0:T(8,128)(2,1)} %fusion.9), channel_id=1, source_target_pairs={{0,4},{2,6},{4,0},{6,2},{8,12},{10,14},{12,8},{14,10},{16,20},{18,... | collective-permute-start | bytes 3538952 | tf_op jit(solution)/shard_map/ppermute | solution.py:157
  360.8 52.1 %collective-permute-start.27 = (bf16[4,576,256]{2,1,0:T(8,128)(2,1)S(1)}, bf16[4,576,256]{2,1,0:T(8,128)(2,1)}, u32[]{:S(2)}, u32[]{:S(2)}) collective-permute-start(bf16[4,576,256]{2,1,0:T(8,128)(2,1)S(1)} %fusion.8), channel_id=1, source_target_pairs={{0,4},{2,6},{4,0},{6,2},{8,12},{10,14},{12,8},{14,10},{16,20},{18,... | collective-permute-start | bytes 3538952 | tf_op jit(solution)/shard_map/ppermute | solution.py:157
  373.7 56.8 %collective-permute-start.20 = (bf16[4,576,256]{2,1,0:T(8,128)(2,1)S(1)}, bf16[4,576,256]{2,1,0:T(8,128)(2,1)S(1)}, u32[]{:S(2)}, u32[]{:S(2)}) collective-permute-start(bf16[4,576,256]{2,1,0:T(8,128)(2,1)S(1)} %fusion.7), channel_id=1, source_target_pairs={{0,4},{2,6},{4,0},{6,2},{8,12},{10,14},{12,8},{14,10},{16,20},{18,... | collective-permute-start | bytes 3538952 | tf_op jit(solution)/shard_map/ppermute | solution.py:157
  376.9 54.7 %collective-permute-start.42 = (bf16[576,256]{1,0:T(8,128)(2,1)S(1)}, bf16[576,256]{1,0:T(8,128)(2,1)S(1)}, u32[]{:S(2)}, u32[]{:S(2)}) collective-permute-start(bf16[576,256]{1,0:T(8,128)(2,1)S(1)} %get-tuple-element.33), channel_id=1, source_target_pairs={{0,8},{2,10},{4,12},{6,14},{1,9},{3,11},{5,13},{7,15}} | collective-permute-start | bytes 884744 | tf_op jit(solution)/shard_map/ppermute | solution.py:47
  387.6 67.5 %collective-permute-start.45 = (bf16[576,256]{1,0:T(8,128)(2,1)S(1)}, bf16[576,256]{1,0:T(8,128)(2,1)S(1)}, u32[]{:S(2)}, u32[]{:S(2)}) collective-permute-start(bf16[576,256]{1,0:T(8,128)(2,1)S(1)} %get-tuple-element.34), channel_id=1, source_target_pairs={{24,16},{26,18},{28,20},{30,22},{25,17},{27,19},{29,21},{31,23}} | collective-permute-start | bytes 884744 | tf_op jit(solution)/shard_map/ppermute | solution.py:48
  430.5 31.0 %collective-permute-start.38 = (bf16[576,256]{1,0:T(8,128)(2,1)S(1)}, bf16[576,256]{1,0:T(8,128)(2,1)S(1)}, u32[]{:S(2)}, u32[]{:S(2)}) collective-permute-start(bf16[576,256]{1,0:T(8,128)(2,1)S(1)} %get-tuple-element.30), channel_id=1, source_target_pairs={{24,16},{26,18},{28,20},{30,22},{25,17},{27,19},{29,21},{31,23}} | collective-permute-start | bytes 884744 | tf_op jit(solution)/shard_map/ppermute | solution.py:48
  474.8 29.1 %collective-permute-start.37 = (bf16[576,256]{1,0:T(8,128)(2,1)S(1)}, bf16[576,256]{1,0:T(8,128)(2,1)S(1)}, u32[]{:S(2)}, u32[]{:S(2)}) collective-permute-start(bf16[576,256]{1,0:T(8,128)(2,1)S(1)} %get-tuple-element.27), channel_id=1, source_target_pairs={{0,8},{2,10},{4,12},{6,14},{8,16},{10,18},{12,20},{14,22},{16,24},... | collective-permute-start | bytes 884744 | tf_op jit(solution)/shard_map/ppermute | solution.py:47
  518.1 29.8 %collective-permute-start.48 = (bf16[288,1024]{1,0:T(8,128)(2,1)S(1)}, bf16[288,1024]{1,0:T(8,128)(2,1)S(1)}, u32[]{:S(2)}, u32[]{:S(2)}) collective-permute-start(bf16[288,1024]{1,0:T(8,128)(2,1)S(1)} %fusion.32), channel_id=1, source_target_pairs={{0,2},{2,0},{4,6},{6,4},{8,10},{10,8},{12,14},{14,12},{16,18},{18,... | collective-permute-start | bytes 1769480 | tf_op jit(solution)/shard_map/ppermute | solution.py:171
  (46 other events, 711.0 us)
Sparse Core Ops, SparseCore 0:
  9.6 24.4 all-gather.2
  152.0 21.8 all-gather.4

commit v2 on v1

--- a/solution.py
+++ b/solution.py
@@ -62,11 +62,25 @@
     return lax.dynamic_slice_in_dim(line, nz - 1 - z, nz, 0)
 
 
+def after(value, *others):
+    return lax.optimization_barrier((value,) + others)[0]
+
+
 def in_order(first, own, other, axis):
     return jnp.where(
         first,
         jnp.concatenate([own, other], axis=axis),
         jnp.concatenate([other, own], axis=axis),
+    )
+
+
+def project(block, *parts):
+    return jnp.concatenate(
+        [
+            jnp.dot(block, part, preferred_element_type=jnp.float32).astype(jnp.bfloat16)
+            for part in parts
+        ],
+        axis=1,
     )
 
 
@@ -90,7 +104,7 @@
     features_other = lax.all_gather(grad_other, "tensor", axis=1, tiled=True)
     attn_mine = lax.dynamic_slice_in_dim(attn_out, x * half, half, 1)
     attn_send = lax.dynamic_slice_in_dim(attn_out, (1 - x) * half, half, 1)
-    attn_other = lax.ppermute(attn_send, "dp", x_pairs(n))
+    attn_other = lax.ppermute(after(attn_send, grad_other), "dp", x_pairs(n))
     attn_both = jnp.concatenate([attn_mine, attn_other], axis=0)
 
     cut = embeds.reshape(resp_dev, n, part).transpose(1, 0, 2)
@@ -104,8 +118,8 @@
     ).reshape(nz, NY, NX, resp_dev, 2, hidden_local)
     keep = lax.dynamic_index_in_dim(partial, y, 1, keepdims=False)
     send = lax.dynamic_index_in_dim(partial, 1 - y, 1, keepdims=False)
-    keep = keep + lax.ppermute(send, "dp", y_pairs(n))
-    keep = line_reduce(keep, z, n, jnp.float32)
+    got = lax.ppermute(send, "dp", y_pairs(n))
+    keep = line_reduce(keep + got, z, n, jnp.float32)
     both = at(keep, x) + lax.ppermute(at(keep, 1 - x), "dp", x_pairs(n))
     upper, lower = both[:, 0], both[:, 1]
 
@@ -134,17 +148,22 @@
 
     weighted = jnp.concatenate([scale(features, coef), scale(features_other, coef_other)], axis=0)
 
-    w_other = lax.ppermute(
-        lax.dynamic_slice_in_dim(w_out, (1 - x) * half, half, 1), "dp", x_pairs(n)
-    )
+    w_send = lax.dynamic_slice_in_dim(w_out, (1 - x) * half, half, 1)
+    w_other = lax.ppermute(after(w_send, send), "dp", x_pairs(n))
     w_mine = lax.dynamic_slice_in_dim(w_out, x * half, half, 1)
     w_pair = in_order(x == 0, w_mine, w_other, 0)
-    w_line = line_gather(w_pair, z, n)
-    w_line_other = lax.ppermute(w_line, "dp", y_pairs(n))
-    w_all = in_order(y == 0, w_line[:, None], w_line_other[:, None], 1).reshape(-1, half)
+    w_a, w_b = w_pair[:, : half // 2], w_pair[:, half // 2 :]
+    w_a = line_gather(w_a, z, n)
+    w_a_other = lax.ppermute(after(w_a, got), "dp", y_pairs(n))
+    w_a = in_order(y == 0, w_a[:, None], w_a_other[:, None], 1).reshape(-1, half // 2)
+    w_b_other = lax.ppermute(after(w_b, got), "dp", y_pairs(n))
+    w_b = in_order(y == 0, w_b[None], w_b_other[None], 0)
+    w_b = line_gather(after(w_b, keep), z, n).reshape(-1, half // 2)
 
     step = half // CHUNKS
     pieces = []
+    came = None
+    d_attn = None
     for c in range(CHUNKS):
         block = lax.dot_general(
             weighted,
@@ -154,17 +173,17 @@
         ).reshape(nz, NY, NX * rows_out, step)
         mine = lax.dynamic_index_in_dim(block, y, 1, keepdims=False)
         away = lax.dynamic_index_in_dim(block, 1 - y, 1, keepdims=False).astype(jnp.bfloat16)
-        mine = mine + lax.ppermute(away, "dp", y_pairs(n)).astype(jnp.float32)
-        pieces.append(line_reduce(mine, z, n, jnp.bfloat16))
-
-    d_send = jnp.dot(weighted[tokens:], w_all, preferred_element_type=jnp.float32).astype(
-        jnp.bfloat16
-    )
-    d_other = lax.ppermute(d_send, "dp", x_pairs(n))
-    d_mine = jnp.dot(weighted[:tokens], w_all, preferred_element_type=jnp.float32).astype(
-        jnp.bfloat16
-    )
-    d_attn = in_order(x == 0, d_mine, d_other, 1)
+        if came is not None:
+            away = after(away, came)
+        came = lax.ppermute(away, "dp", y_pairs(n))
+        if c == 0:
+            w_a, w_b, _ = lax.optimization_barrier((w_a, w_b, came))
+            d_other = lax.ppermute(project(weighted[tokens:], w_a, w_b), "dp", x_pairs(n))
+            d_mine = project(weighted[:tokens], w_a, w_b)
+            d_attn = in_order(x == 0, d_mine, d_other, 1)
+        if c == CHUNKS - 1:
+            came, d_attn = lax.optimization_barrier((came, d_attn))
+        pieces.append(line_reduce(mine + came.astype(jnp.float32), z, n, jnp.bfloat16))
 
     total_resp = resp_dev * n
     summed = jnp.concatenate(pieces, axis=1).reshape(NX, rows_out, half)

time: 567 us -> 535 us (0.944)
  local copies, waits for them, and re-layouts: 68.3 us -> 49.4 us
  starting transfers between devices: 132 us -> 115 us
  waiting for transfers between devices: 198 us -> 206 us
  other arithmetic: 66.4 us -> 59.3 us
    ppermute x9 -> x10, waiting for transfers between devices: 137 us -> 51.7 us  [the longest x4 23.3 us: shards(): came = lax.ppermute(away, 'dp', y_pairs(n))]
    ppermute x3 -> x6, waiting for transfers between devices: 0.01 us -> 33.3 us  [line_gather(): left = lax.ppermute(left, 'dp', z_pairs(n, step, -1, True))]
    ppermute x15, starting transfers between devices: 83.9 us -> 52.5 us  [line_reduce(): right = lax.ppermute(give_r.astype(dtype), 'dp', z_pairs(n, step, 1, False))]
    ppermute x3 -> x6, waiting for transfers between devices: 0.01 us -> 17.5 us  [line_gather(): right = lax.ppermute(right, 'dp', z_pairs(n, step, 1, True))]
    ppermute x1, waiting for transfers between devices: 6.98 us -> 23.5 us  [shards(): grad_other = lax.ppermute(grad_out, 'dp', x_pairs(n))]
    ppermute x1, waiting for transfers between devices: 15.7 us -> 30.9 us  [shards(): both = at(keep, x) + lax.ppermute(at(keep, 1 - x), 'dp', x_pairs(n))]
    ppermute x3 -> x6, starting transfers between devices: 7.14 us -> 14.5 us  [line_gather(): right = lax.ppermute(right, 'dp', z_pairs(n, step, 1, True))]
    ppermute x15, waiting for transfers between devices: 9.35 us -> 15.4 us  [line_reduce(): left = lax.ppermute(give_l.astype(dtype), 'dp', z_pairs(n, step, -1, False))]
  transfers between devices with their start and end apart: 52 -> 59, of which waited for: 20 -> 25; matrix products, arithmetic and copies ran while one was open for 36% -> 31% of each run, Pallas kernels for 0% -> 0%
where the time goes in v2:
time: 535 us; the launch traced here: 525 us
  waiting for transfers between devices  206 us (39%)
  starting transfers between devices  115 us (21%)
  matrix products  76.9 us (14%)
  other arithmetic  59.3 us (11%)
  local copies, waits for them, and re-layouts  49.4 us (9%)
  between operations  15.6 us (3%)
    ppermute x15, starting transfers between devices, line_reduce(): right = lax.ppermute(give_r.astype(dtype), 'dp', z_pairs(n, step, 1, False))  52.5 us
    dot_general x4, matrix products, shards(): lax.dot_general(weighted, attn_both[:, c * step:(c + 1) * step], (((0,),...  39.6 us
    dot_general x4, matrix products, project(): jnp.dot(block, part, preferred_element_type=jnp.float32)  33.9 us
    ppermute x6, waiting for transfers between devices, line_gather(): left = lax.ppermute(left, 'dp', z_pairs(n, step, -1, True))  33.3 us
    ppermute x1, waiting for transfers between devices, shards(): both = at(keep, x) + lax.ppermute(at(keep, 1 - x), 'dp', x_pairs(n))  30.9 us
    ppermute x1, waiting for transfers between devices, shards(): grad_other = lax.ppermute(grad_out, 'dp', x_pairs(n))  23.5 us
    ppermute x4, waiting for transfers between devices, shards(): came = lax.ppermute(away, 'dp', y_pairs(n))  23.3 us
    ppermute x15, waiting for transfers between devices, line_reduce(): right = lax.ppermute(give_r.astype(dtype), 'dp', z_pairs(n, step, 1, False))  21.3 us
  transfers between devices with their start and end apart: 59, of which 25 were waited for; matrix products, arithmetic and copies ran while one was open for 31% of the time, Pallas kernels for 0%

profile of v2, /device:TPU:0, one launch (start us, length us, event | category | flops | bytes accessed | tf_op | source)
XLA Modules:
  0.0 524.6 jit_solution(11348171761507012660)
XLA Ops:
  9.1 8.3 %all-to-all-start = ((bf16[16,16,288]{2,1,0:T(8,128)(2,1)}), bf16[16,16,288]{2,1,0:T(8,128)(2,1)S(1)}, u32[]{:S(2)}, u32[]{:S(2)}) async-start(bf16[16,16,288]{2,1,0:T(8,128)(2,1)} %bitcast.243), calls=%async_computation | async-start | bytes 393216 | tf_op jit(solution)/shard_map/all_to_all | solution.py:111
  17.6 8.4 %all-to-all-done = bf16[16,16,288]{2,1,0:T(8,128)(2,1)S(1)} async-done(((bf16[16,16,288]{2,1,0:T(8,128)(2,1)}), bf16[16,16,288]{2,1,0:T(8,128)(2,1)S(1)}, u32[]{:S(2)}, u32[]{:S(2)}) %all-to-all-start) | async-done | bytes 147488 | tf_op jit(solution)/shard_map/all_to_all | solution.py:111
  34.2 11.9 %collective-permute-done.15 = bf16[288,1024]{1,0:T(8,128)(2,1)S(1)} collective-permute-done((bf16[288,1024]{1,0:T(8,128)(2,1)S(1)}, bf16[288,1024]{1,0:T(8,128)(2,1)S(1)}, u32[]{:S(2)}, u32[]{:S(2)}) %collective-permute-start.15) | collective-permute-done | bytes 589856 | tf_op jit(solution)/shard_map/ppermute | solution.py:152
  52.9 8.1 %collective-permute-done.16 = bf16[576,512]{1,0:T(8,128)(2,1)S(1)} collective-permute-done((bf16[576,512]{1,0:T(8,128)(2,1)S(1)}, bf16[576,512]{1,0:T(8,128)(2,1)S(1)}, u32[]{:S(2)}, u32[]{:S(2)}) %collective-permute-start.16) | collective-permute-done | bytes 589856 | tf_op jit(solution)/shard_map/ppermute | solution.py:57
  70.8 14.8 %collective-permute-done = f32[4,2,16,2,2304]{4,2,3,1,0:T(8,128)} collective-permute-done((f32[4,2,16,2,2304]{4,2,3,1,0:T(8,128)}, f32[4,2,16,2,2304]{4,2,3,1,0:T(8,128)}, u32[]{:S(2)}, u32[]{:S(2)}) %collective-permute-start) | collective-permute-done | bytes 2359328 | tf_op jit(solution)/shard_map/ppermute | solution.py:121
  108.4 7.7 %collective-permute-done.2 = f32[2,16,2,2304]{3,1,2,0:T(8,128)S(1)} collective-permute-done((f32[2,16,2,2304]{3,1,2,0:T(8,128)S(1)}, f32[2,16,2,2304]{3,1,2,0:T(8,128)S(1)}, u32[]{:S(2)}, u32[]{:S(2)}) %collective-permute-start.2) | collective-permute-done | bytes 589856 | tf_op jit(solution)/shard_map/ppermute | solution.py:47
  128.5 23.5 %collective-permute-done.8 = bf16[1024,2304]{1,0:T(8,128)(2,1)} collective-permute-done((bf16[1024,2304]{1,0:T(8,128)(2,1)}, bf16[1024,2304]{1,0:T(8,128)(2,1)}, u32[]{:S(2)}, u32[]{:S(2)}) %collective-permute-start.8) | collective-permute-done | bytes 4718624 | tf_op jit(solution)/shard_map/ppermute | solution.py:102
  157.4 10.9 %collective-permute-done.6 = f32[2,16,2,2304]{3,1,2,0:T(8,128)S(1)} collective-permute-done((f32[2,16,2,2304]{3,1,2,0:T(8,128)S(1)}, f32[2,16,2,2304]{3,1,2,0:T(8,128)S(1)}, u32[]{:S(2)}, u32[]{:S(2)}) %collective-permute-start.6) | collective-permute-done | bytes 589856 | tf_op jit(solution)/shard_map/ppermute | solution.py:48
  186.2 9.4 %collective-permute-done.24 = bf16[2,576,512]{2,1,0:T(8,128)(2,1)} collective-permute-done((bf16[2,576,512]{2,1,0:T(8,128)(2,1)S(1)}, bf16[2,576,512]{2,1,0:T(8,128)(2,1)}, u32[]{:S(2)}, u32[]{:S(2)}) %collective-permute-start.24) | collective-permute-done | bytes 1179680 | tf_op jit(solution)/shard_map/ppermute | solution.py:57
  197.4 30.9 %collective-permute-done.7 = f32[16,2,2304]{2,0,1:T(8,128)S(1)} collective-permute-done((f32[16,2,2304]{2,0,1:T(8,128)S(1)}, f32[16,2,2304]{2,0,1:T(8,128)S(1)}, u32[]{:S(2)}, u32[]{:S(2)}) %collective-permute-start.7) | collective-permute-done | bytes 294944 | tf_op jit(solution)/shard_map/ppermute | solution.py:123
  240.8 16.2 %collective-permute-done.28 = bf16[2,576,512]{2,1,0:T(8,128)(2,1)} collective-permute-done((bf16[2,576,512]{2,1,0:T(8,128)(2,1)}, bf16[2,576,512]{2,1,0:T(8,128)(2,1)}, u32[]{:S(2)}, u32[]{:S(2)}) %collective-permute-start.28) | collective-permute-done | bytes 1179680 | tf_op jit(solution)/shard_map/ppermute | solution.py:58
  265.6 16.6 %collective-permute-done.29 = bf16[2,576,512]{2,1,0:T(8,128)(2,1)S(1)} collective-permute-done((bf16[2,576,512]{2,1,0:T(8,128)(2,1)}, bf16[2,576,512]{2,1,0:T(8,128)(2,1)S(1)}, u32[]{:S(2)}, u32[]{:S(2)}) %collective-permute-start.29) | collective-permute-done | bytes 1179680 | tf_op jit(solution)/shard_map/ppermute | solution.py:58
  284.8 10.4 %multiply_convert_fusion.1 = bf16[1024,4608]{1,0:T(8,128)(2,1)} fusion(bf16[1024,4608]{1,0:T(8,128)(2,1)} %all-gather.3.cloned.1.call-done, f32[1024]{0:T(1024)S(1)} %mul.130), kind=kLoop, calls=%fused_computation.6 | loop fusion | flops 14155776 | bytes 18878464 | tf_op jit(solution)/shard_map/convert_element_type | solution.py:147
  295.2 10.7 %multiply_convert_fusion = bf16[1024,4608]{1,0:T(8,128)(2,1)} fusion(bf16[1024,4608]{1,0:T(8,128)(2,1)} %all-gather.5.cloned.1.call-done, f32[1024]{0:T(1024)S(1)} %mul.134), kind=kLoop, calls=%fused_computation.5 | loop fusion | flops 14155776 | bytes 18878464 | tf_op jit(solution)/shard_map/convert_element_type | solution.py:147
  305.9 11.1 %fusion.20 = f32[4608,256]{1,0:T(8,128)} fusion(bf16[1024,1024]{1,0:T(8,128)(2,1)} %collective-permute-done.10, bf16[1024,1024]{1,0:T(8,128)(2,1)} %get-tuple-element.42, bf16[1024,4608]{1,0:T(8,128)(2,1)} %multiply_convert_fusion, bf16[1024,4608]{1,0:T(8,128)(2,1)} %multiply_convert_fusion.1), kind=kOutput, calls=%fused_computation.68 | convolution fusion | flops 4871684096 | bytes 27787264 | tf_op jit(solution)/shard_map/dot_general | solution.py:168
  319.9 9.5 %fusion.12 = f32[4608,256]{1,0:T(8,128)} fusion(bf16[1024,1024]{1,0:T(8,128)(2,1)} %get-tuple-element.42, bf16[1024,1024]{1,0:T(8,128)(2,1)} %collective-permute-done.10, bf16[1024,4608]{1,0:T(8,128)(2,1)} %multiply_convert_fusion, bf16[1024,4608]{1,0:T(8,128)(2,1)S(1)} %bitcast.245), kind=kOutput, calls=%fused_computation.62 | convolution fusion | flops 4871684096 | bytes 27787264 | tf_op jit(solution)/shard_map/dot_general | solution.py:168
  329.4 9.5 %fusion.18 = f32[4608,256]{1,0:T(8,128)} fusion(bf16[1024,1024]{1,0:T(8,128)(2,1)} %get-tuple-element.42, bf16[1024,1024]{1,0:T(8,128)(2,1)} %collective-permute-done.10, bf16[1024,4608]{1,0:T(8,128)(2,1)} %multiply_convert_fusion, bf16[1024,4608]{1,0:T(8,128)(2,1)S(1)} %bitcast.245), kind=kOutput, calls=%fused_computation.66 | convolution fusion | flops 4871684096 | bytes 27787264 | tf_op jit(solution)/shard_map/dot_general | solution.py:168
  338.9 9.5 %fusion.15 = f32[4608,256]{1,0:T(8,128)} fusion(bf16[1024,1024]{1,0:T(8,128)(2,1)} %get-tuple-element.42, bf16[1024,1024]{1,0:T(8,128)(2,1)} %collective-permute-done.10, bf16[1024,4608]{1,0:T(8,128)(2,1)} %multiply_convert_fusion, bf16[1024,4608]{1,0:T(8,128)(2,1)S(1)} %bitcast.245), kind=kOutput, calls=%fused_computation.64 | convolution fusion | flops 4871684096 | bytes 27787264 | tf_op jit(solution)/shard_map/dot_general | solution.py:168
  359.7 7.9 %convolution_convert_fusion.3 = bf16[1024,512]{0,1:T(8,128)(2,1)} fusion(bf16[1024,4608]{1,0:T(8,128)(2,1)S(1)} %bitcast.245, bf16[4608,512]{1,0:T(8,128)(2,1)} %bitcast.248), kind=kOutput, calls=%fused_computation.41 | convolution fusion | flops 4832362496 | bytes 15204352 | tf_op jit(solution)/shard_map/dot_general | solution.py:80
  369.1 8.9 %convolution_convert_fusion.1 = bf16[1024,512]{0,1:T(8,128)(2,1)} fusion(bf16[1024,4608]{1,0:T(8,128)(2,1)} %multiply_convert_fusion, bf16[4608,512]{1,0:T(8,128)(2,1)S(1)} %bitcast.251), kind=kOutput, calls=%fused_computation.39 | convolution fusion | flops 4832362496 | bytes 15204352 | tf_op jit(solution)/shard_map/dot_general | solution.py:80
  381.0 10.9 %convolution_convert_fusion = bf16[1024,512]{0,1:T(8,128)(2,1)} fusion(bf16[1024,4608]{1,0:T(8,128)(2,1)} %multiply_convert_fusion, bf16[4608,512]{1,0:T(8,128)(2,1)} %bitcast.252), kind=kOutput, calls=%fused_computation.38 | convolution fusion | flops 4832362496 | bytes 15204352 | tf_op jit(solution)/shard_map/dot_general | solution.py:80
  415.1 15.4 %collective-permute-done.13 = bf16[4,576,256]{2,1,0:T(8,128)(2,1)} collective-permute-done((bf16[4,576,256]{2,1,0:T(8,128)(2,1)S(1)}, bf16[4,576,256]{2,1,0:T(8,128)(2,1)}, u32[]{:S(2)}, u32[]{:S(2)}) %collective-permute-start.13) | collective-permute-done | bytes 1179680 | tf_op jit(solution)/shard_map/ppermute | solution.py:178
  487.2 8.9 %collective-permute-start.51 = (bf16[576,256]{1,0:T(8,128)(2,1)S(1)}, bf16[576,256]{1,0:T(8,128)(2,1)S(1)}, u32[]{:S(2)}, u32[]{:S(2)}) collective-permute-start(bf16[576,256]{1,0:T(8,128)(2,1)S(1)} %get-tuple-element.55), channel_id=1, source_target_pairs={{0,8},{2,10},{4,12},{6,14},{8,16},{10,18},{12,20},{14,22},{16,24},... | collective-permute-start | bytes 884744 | tf_op jit(solution)/shard_map/ppermute | solution.py:47
  506.9 6.4 %copy.35 = bf16[1024,2048]{1,0:T(8,128)(2,1)} copy(bf16[1024,2048]{0,1:T(8,128)(2,1)} %maximum_select_fusion.1) | data formatting | bytes 8388608
  (271 shorter events, 223.2 us)
Async XLA Ops:
  7.2 277.6 %all-gather.3.cloned.1.call-start = ((), (), s32[]{:S(2)}) async-start(), calls=%async_computation.1 | async-start | bytes 14155776 | tf_op jit(solution)/shard_map/all_gather | solution.py:103
  17.4 277.8 %all-gather.5.cloned.1.call-start = ((), (), s32[]{:S(2)}) async-start(), calls=%async_computation.2 | async-start | bytes 14155776 | tf_op jit(solution)/shard_map/all_gather | solution.py:104
  33.7 52.0 %collective-permute-start = (f32[4,2,16,2,2304]{4,2,3,1,0:T(8,128)}, f32[4,2,16,2,2304]{4,2,3,1,0:T(8,128)}, u32[]{:S(2)}, u32[]{:S(2)}) collective-permute-start(f32[4,2,16,2,2304]{4,2,3,1,0:T(8,128)} %bitcast.242), channel_id=1, source_target_pairs={{0,4},{2,6},{4,0},{6,2},{8,12},{10,14},{12,8},{14,10},{16,20},{18,... | collective-permute-start | bytes 7077896 | tf_op jit(solution)/shard_map/ppermute | solution.py:121
  50.8 101.2 %collective-permute-start.8 = (bf16[1024,2304]{1,0:T(8,128)(2,1)}, bf16[1024,2304]{1,0:T(8,128)(2,1)}, u32[]{:S(2)}, u32[]{:S(2)}) collective-permute-start(bf16[1024,2304]{1,0:T(8,128)(2,1)} %param.20), channel_id=1, source_target_pairs={{0,2},{2,0},{4,6},{6,4},{8,10},{10,8},{12,14},{14,12},{16,18},{18,... | collective-permute-start | bytes 14155784 | tf_op jit(solution)/shard_map/ppermute | solution.py:102
  68.0 25.4 %collective-permute-start.20 = (bf16[576,512]{1,0:T(8,128)(2,1)}, bf16[576,512]{1,0:T(8,128)(2,1)}, u32[]{:S(2)}, u32[]{:S(2)}) collective-permute-start(bf16[576,512]{1,0:T(8,128)(2,1)} %collective-permute-done.19), channel_id=1, source_target_pairs={{8,0},{10,2},{12,4},{14,6},{16,8},{18,10},{20,12},{22,14},{9,1},{1... | collective-permute-start | bytes 1769480 | tf_op jit(solution)/shard_map/ppermute | solution.py:58
  69.3 26.3 %collective-permute-start.18 = (bf16[576,512]{1,0:T(8,128)(2,1)}, bf16[576,512]{1,0:T(8,128)(2,1)}, u32[]{:S(2)}, u32[]{:S(2)}) collective-permute-start(bf16[576,512]{1,0:T(8,128)(2,1)} %collective-permute-done.17), channel_id=1, source_target_pairs={{16,24},{18,26},{20,28},{22,30},{17,25},{19,27},{21,29},{23,31}} | collective-permute-start | bytes 1769480 | tf_op jit(solution)/shard_map/ppermute | solution.py:57
  93.5 25.5 %collective-permute-start.21 = (bf16[576,512]{1,0:T(8,128)(2,1)}, bf16[576,512]{1,0:T(8,128)(2,1)S(1)}, u32[]{:S(2)}, u32[]{:S(2)}) collective-permute-start(bf16[576,512]{1,0:T(8,128)(2,1)} %collective-permute-done.20), channel_id=1, source_target_pairs={{8,0},{10,2},{12,4},{14,6},{9,1},{11,3},{13,5},{15,7}} | collective-permute-start | bytes 1769480 | tf_op jit(solution)/shard_map/ppermute | solution.py:58
  95.6 59.8 %collective-permute-start.23 = (bf16[576,512]{1,0:T(8,128)(2,1)}, bf16[576,512]{1,0:T(8,128)(2,1)}, u32[]{:S(2)}, u32[]{:S(2)}) collective-permute-start(bf16[576,512]{1,0:T(8,128)(2,1)} %get-tuple-element.21), channel_id=1, source_target_pairs={{0,4},{2,6},{4,0},{6,2},{8,12},{10,14},{12,8},{14,10},{16,20},{18,... | collective-permute-start | bytes 1769480 | tf_op jit(solution)/shard_map/ppermute | solution.py:159
  117.2 35.0 %collective-permute-start.5 = (f32[2,16,2,2304]{3,1,2,0:T(8,128)S(1)}, f32[2,16,2,2304]{3,1,2,0:T(8,128)S(1)}, u32[]{:S(2)}, u32[]{:S(2)}) collective-permute-start(f32[2,16,2,2304]{3,1,2,0:T(8,128)S(1)} %get-tuple-element.60), channel_id=1, source_target_pairs={{16,8},{18,10},{20,12},{22,14},{24,16},{26,18},{28,20},{30,22},{17... | collective-permute-start | bytes 1769480 | tf_op jit(solution)/shard_map/ppermute | solution.py:48
  121.8 58.8 %collective-permute-start.22 = (bf16[4,576,512]{2,1,0:T(8,128)(2,1)}, bf16[4,576,512]{2,1,0:T(8,128)(2,1)}, u32[]{:S(2)}, u32[]{:S(2)}) collective-permute-start(bf16[4,576,512]{2,1,0:T(8,128)(2,1)} %constant_dynamic-slice_fusion.1), channel_id=1, source_target_pairs={{0,4},{2,6},{4,0},{6,2},{8,12},{10,14},{12,8},{14,10},{16,20},{18,... | collective-permute-start | bytes 7077896 | tf_op jit(solution)/shard_map/ppermute | solution.py:157
  122.7 34.6 %collective-permute-start.3 = (f32[2,16,2,2304]{3,1,2,0:T(8,128)}, f32[2,16,2,2304]{3,1,2,0:T(8,128)}, u32[]{:S(2)}, u32[]{:S(2)}) collective-permute-start(f32[2,16,2,2304]{3,1,2,0:T(8,128)} %get-tuple-element.59), channel_id=1, source_target_pairs={{0,8},{2,10},{4,12},{6,14},{8,16},{10,18},{12,20},{14,22},{16,24},... | collective-permute-start | bytes 1769480 | tf_op jit(solution)/shard_map/ppermute | solution.py:47
  169.4 26.2 %collective-permute-start.24 = (bf16[2,576,512]{2,1,0:T(8,128)(2,1)S(1)}, bf16[2,576,512]{2,1,0:T(8,128)(2,1)}, u32[]{:S(2)}, u32[]{:S(2)}) collective-permute-start(bf16[2,576,512]{2,1,0:T(8,128)(2,1)S(1)} %maximum_select_fusion.4), channel_id=1, source_target_pairs={{0,8},{2,10},{4,12},{6,14},{8,16},{10,18},{12,20},{14,22},{16,24},... | collective-permute-start | bytes 3538952 | tf_op jit(solution)/shard_map/ppermute | solution.py:57
  177.1 128.8 %collective-permute-start.10 = (bf16[1024,1024]{1,0:T(8,128)(2,1)}, bf16[1024,1024]{1,0:T(8,128)(2,1)}, u32[]{:S(2)}, u32[]{:S(2)}) collective-permute-start(bf16[1024,1024]{1,0:T(8,128)(2,1)} %get-tuple-element.15), channel_id=1, source_target_pairs={{0,2},{2,0},{4,6},{6,4},{8,10},{10,8},{12,14},{14,12},{16,18},{18,... | collective-permute-start | bytes 6291464 | tf_op jit(solution)/shard_map/ppermute | solution.py:107
  179.1 51.6 %collective-permute-start.27 = (bf16[2,576,512]{2,1,0:T(8,128)(2,1)S(1)}, bf16[2,576,512]{2,1,0:T(8,128)(2,1)}, u32[]{:S(2)}, u32[]{:S(2)}) collective-permute-start(bf16[2,576,512]{2,1,0:T(8,128)(2,1)S(1)} %maximum_select_fusion.4), channel_id=1, source_target_pairs={{8,0},{10,2},{12,4},{14,6},{16,8},{18,10},{20,12},{22,14},{24,16},... | collective-permute-start | bytes 3538952 | tf_op jit(solution)/shard_map/ppermute | solution.py:58
  180.4 47.9 %collective-permute-start.7 = (f32[16,2,2304]{2,0,1:T(8,128)S(1)}, f32[16,2,2304]{2,0,1:T(8,128)S(1)}, u32[]{:S(2)}, u32[]{:S(2)}) collective-permute-start(f32[16,2,2304]{2,0,1:T(8,128)S(1)} %dynamic-slice_bitcast_fusion.3), channel_id=1, source_target_pairs={{0,2},{2,0},{4,6},{6,4},{8,10},{10,8},{12,14},{14,12},{16,18},{18,... | collective-permute-start | bytes 884744 | tf_op jit(solution)/shard_map/ppermute | solution.py:123
  195.6 36.4 %collective-permute-start.25 = (bf16[2,576,512]{2,1,0:T(8,128)(2,1)}, bf16[2,576,512]{2,1,0:T(8,128)(2,1)}, u32[]{:S(2)}, u32[]{:S(2)}) collective-permute-start(bf16[2,576,512]{2,1,0:T(8,128)(2,1)} %collective-permute-done.24), channel_id=1, source_target_pairs={{8,16},{10,18},{12,20},{14,22},{16,24},{18,26},{20,28},{22,30},{9,... | collective-permute-start | bytes 3538952 | tf_op jit(solution)/shard_map/ppermute | solution.py:57
  230.7 26.3 %collective-permute-start.28 = (bf16[2,576,512]{2,1,0:T(8,128)(2,1)}, bf16[2,576,512]{2,1,0:T(8,128)(2,1)}, u32[]{:S(2)}, u32[]{:S(2)}) collective-permute-start(bf16[2,576,512]{2,1,0:T(8,128)(2,1)} %collective-permute-done.27), channel_id=1, source_target_pairs={{8,0},{10,2},{12,4},{14,6},{16,8},{18,10},{20,12},{22,14},{9,1},{1... | collective-permute-start | bytes 3538952 | tf_op jit(solution)/shard_map/ppermute | solution.py:58
  232.0 26.7 %collective-permute-start.26 = (bf16[2,576,512]{2,1,0:T(8,128)(2,1)}, bf16[2,576,512]{2,1,0:T(8,128)(2,1)}, u32[]{:S(2)}, u32[]{:S(2)}) collective-permute-start(bf16[2,576,512]{2,1,0:T(8,128)(2,1)} %collective-permute-done.25), channel_id=1, source_target_pairs={{16,24},{18,26},{20,28},{22,30},{17,25},{19,27},{21,29},{23,31}} | collective-permute-start | bytes 3538952 | tf_op jit(solution)/shard_map/ppermute | solution.py:57
  319.8 34.9 %collective-permute-start.11 = (bf16[4,576,256]{2,1,0:T(8,128)(2,1)}, bf16[4,576,256]{2,1,0:T(8,128)(2,1)}, u32[]{:S(2)}, u32[]{:S(2)}) collective-permute-start(bf16[4,576,256]{2,1,0:T(8,128)(2,1)} %fusion.10), channel_id=1, source_target_pairs={{0,4},{2,6},{4,0},{6,2},{8,12},{10,14},{12,8},{14,10},{16,20},{18,... | collective-permute-start | bytes 3538952 | tf_op jit(solution)/shard_map/ppermute | solution.py:178
  378.0 25.9 %collective-permute-start.12 = (bf16[4,576,256]{2,1,0:T(8,128)(2,1)}, bf16[4,576,256]{2,1,0:T(8,128)(2,1)}, u32[]{:S(2)}, u32[]{:S(2)}) collective-permute-start(bf16[4,576,256]{2,1,0:T(8,128)(2,1)} %fusion.9), channel_id=1, source_target_pairs={{0,4},{2,6},{4,0},{6,2},{8,12},{10,14},{12,8},{14,10},{16,20},{18,... | collective-permute-start | bytes 3538952 | tf_op jit(solution)/shard_map/ppermute | solution.py:178
  395.0 41.4 %collective-permute-start.30 = (bf16[1024,1024]{0,1:T(8,128)(2,1)}, bf16[1024,1024]{0,1:T(8,128)(2,1)}, u32[]{:S(2)}, u32[]{:S(2)}) collective-permute-start(bf16[1024,1024]{0,1:T(8,128)(2,1)} %pad_maximum_fusion.2), channel_id=1, source_target_pairs={{0,2},{2,0},{4,6},{6,4},{8,10},{10,8},{12,14},{14,12},{16,18},{18,... | collective-permute-start | bytes 6291464 | tf_op jit(solution)/shard_map/ppermute | solution.py:181
  403.9 26.6 %collective-permute-start.13 = (bf16[4,576,256]{2,1,0:T(8,128)(2,1)S(1)}, bf16[4,576,256]{2,1,0:T(8,128)(2,1)}, u32[]{:S(2)}, u32[]{:S(2)}) collective-permute-start(bf16[4,576,256]{2,1,0:T(8,128)(2,1)S(1)} %fusion.8), channel_id=1, source_target_pairs={{0,4},{2,6},{4,0},{6,2},{8,12},{10,14},{12,8},{14,10},{16,20},{18,... | collective-permute-start | bytes 3538952 | tf_op jit(solution)/shard_map/ppermute | solution.py:178
  433.9 27.6 %collective-permute-start.40 = (bf16[576,256]{1,0:T(8,128)(2,1)S(1)}, bf16[576,256]{1,0:T(8,128)(2,1)S(1)}, u32[]{:S(2)}, u32[]{:S(2)}) collective-permute-start(bf16[576,256]{1,0:T(8,128)(2,1)S(1)} %get-tuple-element.50), channel_id=1, source_target_pairs={{24,16},{26,18},{28,20},{30,22},{25,17},{27,19},{29,21},{31,23}} | collective-permute-start | bytes 884744 | tf_op jit(solution)/shard_map/ppermute | solution.py:48
  467.9 28.3 %collective-permute-start.39 = (bf16[576,256]{1,0:T(8,128)(2,1)S(1)}, bf16[576,256]{1,0:T(8,128)(2,1)S(1)}, u32[]{:S(2)}, u32[]{:S(2)}) collective-permute-start(bf16[576,256]{1,0:T(8,128)(2,1)S(1)} %get-tuple-element.47), channel_id=1, source_target_pairs={{0,8},{2,10},{4,12},{6,14},{8,16},{10,18},{12,20},{14,22},{16,24},... | collective-permute-start | bytes 884744 | tf_op jit(solution)/shard_map/ppermute | solution.py:47
  (62 other events, 907.5 us)
Sparse Core Ops, SparseCore 0:
  9.6 24.4 all-gather.2
  152.2 22.2 all-gather.4

commit v3 on v2

--- a/solution.py
+++ b/solution.py
@@ -6,7 +6,7 @@
 eta_scale = 2.0
 NX = 2
 NY = 2
-CHUNKS = 4
+CHUNKS = (3, 2, 2, 1)
 
 
 def x_pairs(n):
@@ -35,6 +35,11 @@
     return lax.dynamic_index_in_dim(array, index, 0, keepdims=False)
 
 
+def after(value, *others):
+    marks = tuple(other[(slice(0, 1),) * other.ndim] for other in others)
+    return lax.optimization_barrier((value,) + marks)[0]
+
+
 def line_reduce(own, z, n, dtype):
     nz = own.shape[0]
     right = left = None
@@ -49,21 +54,19 @@
     return at(own, z) + right.astype(jnp.float32) + left.astype(jnp.float32)
 
 
-def line_gather(own, z, n):
+def line_gather(own, z, n, gates=None):
     nz = n // (NX * NY)
     rights, lefts = [], []
     right = left = own
     for step in range(1, nz):
         right = lax.ppermute(right, "dp", z_pairs(n, step, 1, True))
         left = lax.ppermute(left, "dp", z_pairs(n, step, -1, True))
+        if gates and step in gates:
+            right, left = after(right, gates[step]), after(left, gates[step])
         rights.append(right)
         lefts.append(left)
     line = jnp.stack(rights[::-1] + [own] + lefts)
     return lax.dynamic_slice_in_dim(line, nz - 1 - z, nz, 0)
-
-
-def after(value, *others):
-    return lax.optimization_barrier((value,) + others)[0]
 
 
 def in_order(first, own, other, axis):
@@ -101,11 +104,8 @@
 
     grad_other = lax.ppermute(grad_out, "dp", x_pairs(n))
     features = lax.all_gather(grad_out, "tensor", axis=1, tiled=True)
-    features_other = lax.all_gather(grad_other, "tensor", axis=1, tiled=True)
     attn_mine = lax.dynamic_slice_in_dim(attn_out, x * half, half, 1)
     attn_send = lax.dynamic_slice_in_dim(attn_out, (1 - x) * half, half, 1)
-    attn_other = lax.ppermute(after(attn_send, grad_other), "dp", x_pairs(n))
-    attn_both = jnp.concatenate([attn_mine, attn_other], axis=0)
 
     cut = embeds.reshape(resp_dev, n, part).transpose(1, 0, 2)
     cut = lax.all_to_all(cut, "dp", 0, 0, tiled=True).reshape(n * resp_dev, part)
@@ -120,7 +120,11 @@
     send = lax.dynamic_index_in_dim(partial, 1 - y, 1, keepdims=False)
     got = lax.ppermute(send, "dp", y_pairs(n))
     keep = line_reduce(keep + got, z, n, jnp.float32)
-    both = at(keep, x) + lax.ppermute(at(keep, 1 - x), "dp", x_pairs(n))
+    last = lax.ppermute(at(keep, 1 - x), "dp", x_pairs(n))
+    both = at(keep, x) + last
+    features_other = lax.all_gather(after(grad_other, last), "tensor", axis=1, tiled=True)
+    attn_other = lax.ppermute(after(attn_send, last), "dp", x_pairs(n))
+    attn_both = jnp.concatenate([attn_mine, attn_other], axis=0)
     upper, lower = both[:, 0], both[:, 1]
 
     base = (jnp.arange(prompts_dev, dtype=jnp.int32) * groups)[:, None]
@@ -158,30 +162,35 @@
     w_a = in_order(y == 0, w_a[:, None], w_a_other[:, None], 1).reshape(-1, half // 2)
     w_b_other = lax.ppermute(after(w_b, got), "dp", y_pairs(n))
     w_b = in_order(y == 0, w_b[None], w_b_other[None], 0)
-    w_b = line_gather(after(w_b, keep), z, n).reshape(-1, half // 2)
-
-    step = half // CHUNKS
+
+    unit = half // sum(CHUNKS)
     pieces = []
-    came = None
+    arrivals = []
+    begin = 0
     d_attn = None
-    for c in range(CHUNKS):
+    for c, units in enumerate(CHUNKS):
+        step = units * unit
         block = lax.dot_general(
             weighted,
-            attn_both[:, c * step : (c + 1) * step],
+            attn_both[:, begin : begin + step],
             (((0,), (0,)), ((), ())),
             preferred_element_type=jnp.float32,
         ).reshape(nz, NY, NX * rows_out, step)
         mine = lax.dynamic_index_in_dim(block, y, 1, keepdims=False)
         away = lax.dynamic_index_in_dim(block, 1 - y, 1, keepdims=False).astype(jnp.bfloat16)
-        if came is not None:
-            away = after(away, came)
+        begin += step
+        if c >= 2:
+            away = after(away, arrivals[c - 2])
         came = lax.ppermute(away, "dp", y_pairs(n))
+        arrivals.append(came)
         if c == 0:
-            w_a, w_b, _ = lax.optimization_barrier((w_a, w_b, came))
+            gates = {1: last, nz - 2: weighted, nz - 1: came}
+            w_a = after(w_a, came)
+            w_b = line_gather(after(w_b, keep), z, n, gates).reshape(-1, half // 2)
             d_other = lax.ppermute(project(weighted[tokens:], w_a, w_b), "dp", x_pairs(n))
             d_mine = project(weighted[:tokens], w_a, w_b)
             d_attn = in_order(x == 0, d_mine, d_other, 1)
-        if c == CHUNKS - 1:
+        if c == len(CHUNKS) - 1:
             came, d_attn = lax.optimization_barrier((came, d_attn))
         pieces.append(line_reduce(mine + came.astype(jnp.float32), z, n, jnp.bfloat16))
 

time: 535 us -> 691 us (1.29)
  waiting for transfers between devices: 206 us -> 325 us
  local copies, waits for them, and re-layouts: 49.4 us -> 68.7 us
  starting transfers between devices: 115 us -> 127 us
    ppermute x1, waiting for transfers between devices: 11.9 us -> 96.9 us  [shards(): w_other = lax.ppermute(after(w_send, send), 'dp', x_pairs(n))]
    ppermute x1, waiting for transfers between devices: 0.01 us -> 49.3 us  [shards(): w_b_other = lax.ppermute(after(w_b, got), 'dp', y_pairs(n))]
    ppermute x1, waiting for transfers between devices: 14.8 us -> 50.3 us  [shards(): got = lax.ppermute(send, 'dp', y_pairs(n))]
    ppermute x1, waiting for transfers between devices: 23.5 us -> 0.01 us  [shards(): grad_other = lax.ppermute(grad_out, 'dp', x_pairs(n))]
    ppermute x2, waiting for transfers between devices: 30.9 us -> 9 us  [the longest x1 4.81 us: shards(): last = lax.ppermute(at(keep, 1 - x), 'dp', x_pairs(n))]
    ppermute x6, waiting for transfers between devices: 33.3 us -> 16 us  [line_gather(): left = lax.ppermute(left, 'dp', z_pairs(n, step, -1, True))]
    ppermute x4, waiting for transfers between devices: 23.3 us -> 39.8 us  [shards(): came = lax.ppermute(away, 'dp', y_pairs(n))]
    ppermute x6, waiting for transfers between devices: 17.5 us -> 2.96 us  [line_gather(): right = lax.ppermute(right, 'dp', z_pairs(n, step, 1, True))]
  transfers between devices with their start and end apart: 59 -> 59, of which waited for: 25 -> 21; matrix products, arithmetic and copies ran while one was open for 31% -> 29% of each run, Pallas kernels for 0% -> 0%
where the time goes in v3:
time: 691 us; the launch traced here: 681 us
  waiting for transfers between devices  325 us (47%)
  starting transfers between devices  127 us (18%)
  matrix products  79.8 us (12%)
  local copies, waits for them, and re-layouts  68.7 us (10%)
  other arithmetic  62.4 us (9%)
  between operations  15.3 us (2%)
    ppermute x1, waiting for transfers between devices, shards(): w_other = lax.ppermute(after(w_send, send), 'dp', x_pairs(n))  96.9 us
    ppermute x15, starting transfers between devices, line_reduce(): right = lax.ppermute(give_r.astype(dtype), 'dp', z_pairs(n, step, 1, False))  55.7 us
    ppermute x1, waiting for transfers between devices, shards(): got = lax.ppermute(send, 'dp', y_pairs(n))  50.3 us
    ppermute x1, waiting for transfers between devices, shards(): w_b_other = lax.ppermute(after(w_b, got), 'dp', y_pairs(n))  49.3 us
    dot_general x4, matrix products, shards(): lax.dot_general(weighted, attn_both[:, begin:begin + step], (((0,), (0,))...  46 us
    ppermute x4, waiting for transfers between devices, shards(): came = lax.ppermute(away, 'dp', y_pairs(n))  39.8 us
    dot_general x4, matrix products, project(): jnp.dot(block, part, preferred_element_type=jnp.float32)  31 us
    unnamed x61, local copies, waits for them, and re-layouts  30.9 us
  transfers between devices with their start and end apart: 59, of which 21 were waited for; matrix products, arithmetic and copies ran while one was open for 29% of the time, Pallas kernels for 0%

profile of v3, /device:TPU:0, one launch (start us, length us, event | category | flops | bytes accessed | tf_op | source)
XLA Modules:
  0.0 680.8 jit_solution(12046536381297104267)
XLA Ops:
  9.2 8.3 %all-to-all-start = ((bf16[16,16,288]{2,1,0:T(8,128)(2,1)}), bf16[16,16,288]{2,1,0:T(8,128)(2,1)S(1)}, u32[]{:S(2)}, u32[]{:S(2)}) async-start(bf16[16,16,288]{2,1,0:T(8,128)(2,1)} %bitcast.239), calls=%async_computation | async-start | bytes 393216 | tf_op jit(solution)/shard_map/all_to_all | solution.py:111
  17.7 8.5 %all-to-all-done = bf16[16,16,288]{2,1,0:T(8,128)(2,1)S(1)} async-done(((bf16[16,16,288]{2,1,0:T(8,128)(2,1)}), bf16[16,16,288]{2,1,0:T(8,128)(2,1)S(1)}, u32[]{:S(2)}, u32[]{:S(2)}) %all-to-all-start) | async-done | bytes 147488 | tf_op jit(solution)/shard_map/all_to_all | solution.py:111
  33.4 50.3 %collective-permute-done = f32[4,2,16,2,2304]{4,2,3,1,0:T(8,128)S(1)} collective-permute-done((f32[4,2,16,2,2304]{4,2,3,1,0:T(8,128)}, f32[4,2,16,2,2304]{4,2,3,1,0:T(8,128)S(1)}, u32[]{:S(2)}, u32[]{:S(2)}) %collective-permute-start) | collective-permute-done | bytes 2359328 | tf_op jit(solution)/shard_map/ppermute | solution.py:121
  108.7 96.9 %collective-permute-done.12 = bf16[288,1024]{1,0:T(8,128)(2,1)S(1)} collective-permute-done((bf16[288,1024]{1,0:T(8,128)(2,1)}, bf16[288,1024]{1,0:T(8,128)(2,1)S(1)}, u32[]{:S(2)}, u32[]{:S(2)}) %collective-permute-start.12) | collective-permute-done | bytes 589856 | tf_op jit(solution)/shard_map/ppermute | solution.py:156
  221.7 11.2 %collective-permute-start.3 = (f32[2,16,2,2304]{3,1,2,0:T(8,128)}, f32[2,16,2,2304]{3,1,2,0:T(8,128)}, u32[]{:S(2)}, u32[]{:S(2)}) collective-permute-start(f32[2,16,2,2304]{3,1,2,0:T(8,128)} %get-tuple-element.59), channel_id=1, source_target_pairs={{0,8},{2,10},{4,12},{6,14},{8,16},{10,18},{12,20},{14,22},{16,24},... | collective-permute-start | bytes 1769480 | tf_op jit(solution)/shard_map/ppermute | solution.py:52
  241.5 11.6 %collective-permute-done.6 = f32[2,16,2,2304]{3,1,2,0:T(8,128)} collective-permute-done((f32[2,16,2,2304]{3,1,2,0:T(8,128)}, f32[2,16,2,2304]{3,1,2,0:T(8,128)}, u32[]{:S(2)}, u32[]{:S(2)}) %collective-permute-start.6) | collective-permute-done | bytes 589856 | tf_op jit(solution)/shard_map/ppermute | solution.py:53
  269.3 11.4 %collective-permute-done.18 = bf16[576,512]{1,0:T(8,128)(2,1)S(1)} collective-permute-done((bf16[576,512]{1,0:T(8,128)(2,1)}, bf16[576,512]{1,0:T(8,128)(2,1)S(1)}, u32[]{:S(2)}, u32[]{:S(2)}) %collective-permute-start.18) | collective-permute-done | bytes 589856 | tf_op jit(solution)/shard_map/ppermute | solution.py:63
  296.8 49.3 %collective-permute-done.21 = bf16[576,512]{1,0:T(8,128)(2,1)S(1)} collective-permute-done((bf16[576,512]{1,0:T(8,128)(2,1)S(1)}, bf16[576,512]{1,0:T(8,128)(2,1)S(1)}, u32[]{:S(2)}, u32[]{:S(2)}) %collective-permute-start.21) | collective-permute-done | bytes 589856 | tf_op jit(solution)/shard_map/ppermute | solution.py:163
  353.2 5.8 maximum_select_fusion
  371.8 13.5 %collective-permute-start.23 = (bf16[2,576,512]{2,1,0:T(8,128)(2,1)}, bf16[2,576,512]{2,1,0:T(8,128)(2,1)}, u32[]{:S(2)}, u32[]{:S(2)}) collective-permute-start(bf16[2,576,512]{2,1,0:T(8,128)(2,1)} %collective-permute-done.22), channel_id=1, source_target_pairs={{8,16},{10,18},{12,20},{14,22},{16,24},{18,26},{20,28},{22,30},{9,... | collective-permute-start | bytes 3538952 | tf_op jit(solution)/shard_map/ppermute | solution.py:62
  385.4 10.4 %multiply_convert_fusion.1 = bf16[1024,4608]{1,0:T(8,128)(2,1)} fusion(bf16[1024,4608]{1,0:T(8,128)(2,1)} %all-gather.3.cloned.1.call-done, f32[1024]{0:T(1024)S(1)} %mul.130), kind=kLoop, calls=%fused_computation.6 | loop fusion | flops 14155776 | bytes 18878464 | tf_op jit(solution)/shard_map/convert_element_type | solution.py:151
  403.4 10.6 %multiply_convert_fusion = bf16[1024,4608]{1,0:T(8,128)(2,1)} fusion(bf16[1024,4608]{1,0:T(8,128)(2,1)} %all-gather.5.cloned.1.call-done, f32[1024]{0:T(1024)S(1)} %mul.134), kind=kLoop, calls=%fused_computation.5 | loop fusion | flops 14155776 | bytes 18878464 | tf_op jit(solution)/shard_map/convert_element_type | solution.py:151
  418.2 16.2 %fusion.5 = f32[4608,384]{1,0:T(8,128)} fusion(bf16[1024,1024]{1,0:T(8,128)(2,1)} %get-tuple-element.45, bf16[1024,1024]{1,0:T(8,128)(2,1)} %collective-permute-done.10, bf16[1024,4608]{1,0:T(8,128)(2,1)} %multiply_convert_fusion, bf16[1024,4608]{1,0:T(8,128)(2,1)} %multiply_convert_fusion.1), kind=kOutput, calls=%fused_computation.35 | convolution fusion | flops 7288651776 | bytes 30146560 | tf_op jit(solution)/shard_map/dot_general | solution.py:173
  438.2 11.0 %fusion.14 = f32[4608,256]{1,0:T(8,128)} fusion(bf16[1024,1024]{1,0:T(8,128)(2,1)} %get-tuple-element.45, bf16[1024,1024]{1,0:T(8,128)(2,1)} %collective-permute-done.10, bf16[1024,4608]{1,0:T(8,128)(2,1)} %multiply_convert_fusion, bf16[1024,4608]{1,0:T(8,128)(2,1)} %multiply_convert_fusion.1), kind=kOutput, calls=%fused_computation.61 | convolution fusion | flops 4871684096 | bytes 27787264 | tf_op jit(solution)/shard_map/dot_general | solution.py:173
  453.8 9.5 %fusion.16 = f32[4608,256]{1,0:T(8,128)} fusion(bf16[1024,1024]{1,0:T(8,128)(2,1)} %collective-permute-done.10, bf16[1024,1024]{1,0:T(8,128)(2,1)} %get-tuple-element.45, bf16[1024,4608]{1,0:T(8,128)(2,1)} %multiply_convert_fusion, bf16[1024,4608]{1,0:T(8,128)(2,1)S(1)} %bitcast.241), kind=kOutput, calls=%fused_computation.63 | convolution fusion | flops 4871684096 | bytes 27787264 | tf_op jit(solution)/shard_map/dot_general | solution.py:173
  463.3 39.8 %collective-permute-done.35 = bf16[4,576,256]{2,1,0:T(8,128)(2,1)} collective-permute-done((bf16[4,576,256]{2,1,0:T(8,128)(2,1)}, bf16[4,576,256]{2,1,0:T(8,128)(2,1)}, u32[]{:S(2)}, u32[]{:S(2)}) %collective-permute-start.35) | collective-permute-done | bytes 1179680 | tf_op jit(solution)/shard_map/ppermute | solution.py:184
  508.1 9.3 %fusion.45 = f32[4608,128]{1,0:T(8,128)} fusion(bf16[1024,1024]{1,0:T(8,128)(2,1)} %collective-permute-done.10, bf16[1024,1024]{1,0:T(8,128)(2,1)} %get-tuple-element.45, bf16[1024,4608]{1,0:T(8,128)(2,1)} %multiply_convert_fusion, bf16[1024,4608]{1,0:T(8,128)(2,1)S(1)} %bitcast.241), kind=kOutput, calls=%fused_computation.127 | convolution fusion | flops 2454716416 | bytes 25427968 | tf_op jit(solution)/shard_map/dot_general | solution.py:173
  525.5 7.9 %convolution_convert_fusion.3 = bf16[1024,512]{0,1:T(8,128)(2,1)} fusion(bf16[1024,4608]{1,0:T(8,128)(2,1)S(1)} %bitcast.241, bf16[4608,512]{1,0:T(8,128)(2,1)} %bitcast.244), kind=kOutput, calls=%fused_computation.40 | convolution fusion | flops 4832362496 | bytes 15204352 | tf_op jit(solution)/shard_map/dot_general | solution.py:83
  533.5 8.9 %convolution_convert_fusion.1 = bf16[1024,512]{0,1:T(8,128)(2,1)} fusion(bf16[1024,4608]{1,0:T(8,128)(2,1)} %multiply_convert_fusion, bf16[4608,512]{1,0:T(8,128)(2,1)S(1)} %bitcast.247), kind=kOutput, calls=%fused_computation.38 | convolution fusion | flops 4832362496 | bytes 15204352 | tf_op jit(solution)/shard_map/dot_general | solution.py:83
  560.6 9.0 %convolution_convert_fusion = bf16[1024,512]{0,1:T(8,128)(2,1)} fusion(bf16[1024,4608]{1,0:T(8,128)(2,1)} %multiply_convert_fusion, bf16[4608,512]{1,0:T(8,128)(2,1)S(1)} %bitcast.248), kind=kOutput, calls=%fused_computation.37 | convolution fusion | flops 4832362496 | bytes 15204352 | tf_op jit(solution)/shard_map/dot_general | solution.py:83
  592.9 6.7 collective-permute-done.43
  608.6 5.9 collective-permute-done.30
  651.5 9.9 %collective-permute-done.54 = bf16[576,128]{1,0:T(8,128)(2,1)S(1)} collective-permute-done((bf16[576,128]{1,0:T(8,128)(2,1)S(1)}, bf16[576,128]{1,0:T(8,128)(2,1)S(1)}, u32[]{:S(2)}, u32[]{:S(2)}) %collective-permute-start.54) | collective-permute-done | bytes 147488 | tf_op jit(solution)/shard_map/ppermute | solution.py:53
  661.9 6.4 copy.31
  (262 shorter events, 237.3 us)
Async XLA Ops:
  17.6 367.8 %all-gather.3.cloned.1.call-start = ((), (), s32[]{:S(2)}) async-start(), calls=%async_computation.1 | async-start | bytes 14155776 | tf_op jit(solution)/shard_map/all_gather | solution.py:106
  32.5 51.3 %collective-permute-start = (f32[4,2,16,2,2304]{4,2,3,1,0:T(8,128)}, f32[4,2,16,2,2304]{4,2,3,1,0:T(8,128)S(1)}, u32[]{:S(2)}, u32[]{:S(2)}) collective-permute-start(f32[4,2,16,2,2304]{4,2,3,1,0:T(8,128)} %bitcast.238), channel_id=1, source_target_pairs={{0,4},{2,6},{4,0},{6,2},{8,12},{10,14},{12,8},{14,10},{16,20},{18,... | collective-permute-start | bytes 7077896 | tf_op jit(solution)/shard_map/ppermute | solution.py:121
  33.3 370.1 %all-gather.5.cloned.1.call-start = ((), (), s32[]{:S(2)}) async-start(), calls=%async_computation.2 | async-start | bytes 14155776 | tf_op jit(solution)/shard_map/all_gather | solution.py:125
  92.5 169.8 %collective-permute-start.8 = (bf16[1024,2304]{1,0:T(8,128)(2,1)}, bf16[1024,2304]{1,0:T(8,128)(2,1)}, u32[]{:S(2)}, u32[]{:S(2)}) collective-permute-start(bf16[1024,2304]{1,0:T(8,128)(2,1)} %param.20), channel_id=1, source_target_pairs={{0,2},{2,0},{4,6},{6,4},{8,10},{10,8},{12,14},{14,12},{16,18},{18,... | collective-permute-start | bytes 14155784 | tf_op jit(solution)/shard_map/ppermute | solution.py:105
  94.1 111.5 %collective-permute-start.12 = (bf16[288,1024]{1,0:T(8,128)(2,1)}, bf16[288,1024]{1,0:T(8,128)(2,1)S(1)}, u32[]{:S(2)}, u32[]{:S(2)}) collective-permute-start(bf16[288,1024]{1,0:T(8,128)(2,1)} %get-tuple-element.71), channel_id=1, source_target_pairs={{0,2},{2,0},{4,6},{6,4},{8,10},{10,8},{12,14},{14,12},{16,18},{18,... | collective-permute-start | bytes 1769480 | tf_op jit(solution)/shard_map/ppermute | solution.py:156
  95.6 116.5 %collective-permute-start.4 = (f32[2,16,2,2304]{3,1,2,0:T(8,128)}, f32[2,16,2,2304]{3,1,2,0:T(8,128)}, u32[]{:S(2)}, u32[]{:S(2)}) collective-permute-start(f32[2,16,2,2304]{3,1,2,0:T(8,128)} %get-tuple-element.62), channel_id=1, source_target_pairs={{24,16},{26,18},{28,20},{30,22},{25,17},{27,19},{29,21},{31,23}} | collective-permute-start | bytes 1769480 | tf_op jit(solution)/shard_map/ppermute | solution.py:53
  103.5 108.6 %collective-permute-start.2 = (f32[2,16,2,2304]{3,1,2,0:T(8,128)}, f32[2,16,2,2304]{3,1,2,0:T(8,128)}, u32[]{:S(2)}, u32[]{:S(2)}) collective-permute-start(f32[2,16,2,2304]{3,1,2,0:T(8,128)} %bitcast_add_fusion.22), channel_id=1, source_target_pairs={{0,8},{2,10},{4,12},{6,14},{8,16},{10,18},{12,20},{14,22},{1,9},{3... | collective-permute-start | bytes 1769480 | tf_op jit(solution)/shard_map/ppermute | solution.py:52
  236.1 26.3 %collective-permute-start.17 = (bf16[576,512]{1,0:T(8,128)(2,1)}, bf16[576,512]{1,0:T(8,128)(2,1)}, u32[]{:S(2)}, u32[]{:S(2)}) collective-permute-start(bf16[576,512]{1,0:T(8,128)(2,1)} %collective-permute-done.16), channel_id=1, source_target_pairs={{8,0},{10,2},{12,4},{14,6},{16,8},{18,10},{20,12},{22,14},{9,1},{1... | collective-permute-start | bytes 1769480 | tf_op jit(solution)/shard_map/ppermute | solution.py:63
  237.4 26.3 %collective-permute-start.15 = (bf16[576,512]{1,0:T(8,128)(2,1)}, bf16[576,512]{1,0:T(8,128)(2,1)}, u32[]{:S(2)}, u32[]{:S(2)}) collective-permute-start(bf16[576,512]{1,0:T(8,128)(2,1)} %collective-permute-done.14), channel_id=1, source_target_pairs={{16,24},{18,26},{20,28},{22,30},{17,25},{19,27},{21,29},{23,31}} | collective-permute-start | bytes 1769480 | tf_op jit(solution)/shard_map/ppermute | solution.py:62
  285.0 68.2 %collective-permute-start.19 = (bf16[4,576,512]{2,1,0:T(8,128)(2,1)}, bf16[4,576,512]{2,1,0:T(8,128)(2,1)}, u32[]{:S(2)}, u32[]{:S(2)}) collective-permute-start(bf16[4,576,512]{2,1,0:T(8,128)(2,1)} %constant_dynamic-slice_fusion.1), channel_id=1, source_target_pairs={{0,4},{2,6},{4,0},{6,2},{8,12},{10,14},{12,8},{14,10},{16,20},{18,... | collective-permute-start | bytes 7077896 | tf_op jit(solution)/shard_map/ppermute | solution.py:161
  289.7 56.4 %collective-permute-start.21 = (bf16[576,512]{1,0:T(8,128)(2,1)S(1)}, bf16[576,512]{1,0:T(8,128)(2,1)S(1)}, u32[]{:S(2)}, u32[]{:S(2)}) collective-permute-start(bf16[576,512]{1,0:T(8,128)(2,1)S(1)} %copy-done.13), channel_id=1, source_target_pairs={{0,4},{2,6},{4,0},{6,2},{8,12},{10,14},{12,8},{14,10},{16,20},{18,... | collective-permute-start | bytes 1769480 | tf_op jit(solution)/shard_map/ppermute | solution.py:163
  370.5 47.7 %collective-permute-start.10 = (bf16[1024,1024]{1,0:T(8,128)(2,1)}, bf16[1024,1024]{1,0:T(8,128)(2,1)}, u32[]{:S(2)}, u32[]{:S(2)}) collective-permute-start(bf16[1024,1024]{1,0:T(8,128)(2,1)} %get-tuple-element.18), channel_id=1, source_target_pairs={{0,2},{2,0},{4,6},{6,4},{8,10},{10,8},{12,14},{14,12},{16,18},{18,... | collective-permute-start | bytes 6291464 | tf_op jit(solution)/shard_map/ppermute | solution.py:126
  370.5 30.0 %collective-permute-start.26 = (bf16[2,576,512]{2,1,0:T(8,128)(2,1)}, bf16[2,576,512]{2,1,0:T(8,128)(2,1)}, u32[]{:S(2)}, u32[]{:S(2)}) collective-permute-start(bf16[2,576,512]{2,1,0:T(8,128)(2,1)} %collective-permute-done.25), channel_id=1, source_target_pairs={{8,0},{10,2},{12,4},{14,6},{16,8},{18,10},{20,12},{22,14},{9,1},{1... | collective-permute-start | bytes 3538952 | tf_op jit(solution)/shard_map/ppermute | solution.py:63
  371.8 30.0 %collective-permute-start.23 = (bf16[2,576,512]{2,1,0:T(8,128)(2,1)}, bf16[2,576,512]{2,1,0:T(8,128)(2,1)}, u32[]{:S(2)}, u32[]{:S(2)}) collective-permute-start(bf16[2,576,512]{2,1,0:T(8,128)(2,1)} %collective-permute-done.22), channel_id=1, source_target_pairs={{8,16},{10,18},{12,20},{14,22},{16,24},{18,26},{20,28},{22,30},{9,... | collective-permute-start | bytes 3538952 | tf_op jit(solution)/shard_map/ppermute | solution.py:62
  400.4 133.0 %collective-permute-start.27 = (bf16[2,576,512]{2,1,0:T(8,128)(2,1)}, bf16[2,576,512]{2,1,0:T(8,128)(2,1)}, u32[]{:S(2)}, u32[]{:S(2)}) collective-permute-start(bf16[2,576,512]{2,1,0:T(8,128)(2,1)} %collective-permute-done.26), channel_id=1, source_target_pairs={{8,0},{10,2},{12,4},{14,6},{9,1},{11,3},{13,5},{15,7}} | collective-permute-start | bytes 3538952 | tf_op jit(solution)/shard_map/ppermute | solution.py:63
  401.7 140.6 %collective-permute-start.24 = (bf16[2,576,512]{2,1,0:T(8,128)(2,1)}, bf16[2,576,512]{2,1,0:T(8,128)(2,1)}, u32[]{:S(2)}, u32[]{:S(2)}) collective-permute-start(bf16[2,576,512]{2,1,0:T(8,128)(2,1)} %collective-permute-done.23), channel_id=1, source_target_pairs={{16,24},{18,26},{20,28},{22,30},{17,25},{19,27},{21,29},{23,31}} | collective-permute-start | bytes 3538952 | tf_op jit(solution)/shard_map/ppermute | solution.py:62
  437.9 87.4 %collective-permute-start.20 = (bf16[4,576,384]{2,1,0:T(8,128)(2,1)}, bf16[4,576,384]{2,1,0:T(8,128)(2,1)}, u32[]{:S(2)}, u32[]{:S(2)}) collective-permute-start(bf16[4,576,384]{2,1,0:T(8,128)(2,1)} %fusion.3), channel_id=1, source_target_pairs={{0,4},{2,6},{4,0},{6,2},{8,12},{10,14},{12,8},{14,10},{16,20},{18,... | collective-permute-start | bytes 5308424 | tf_op jit(solution)/shard_map/ppermute | solution.py:184
  452.0 51.0 %collective-permute-start.35 = (bf16[4,576,256]{2,1,0:T(8,128)(2,1)}, bf16[4,576,256]{2,1,0:T(8,128)(2,1)}, u32[]{:S(2)}, u32[]{:S(2)}) collective-permute-start(bf16[4,576,256]{2,1,0:T(8,128)(2,1)} %fusion.11), channel_id=1, source_target_pairs={{0,4},{2,6},{4,0},{6,2},{8,12},{10,14},{12,8},{14,10},{16,20},{18,... | collective-permute-start | bytes 3538952 | tf_op jit(solution)/shard_map/ppermute | solution.py:184
  520.8 59.4 %collective-permute-start.39 = (bf16[576,256]{1,0:T(8,128)(2,1)S(1)}, bf16[576,256]{1,0:T(8,128)(2,1)S(1)}, u32[]{:S(2)}, u32[]{:S(2)}) collective-permute-start(bf16[576,256]{1,0:T(8,128)(2,1)S(1)} %get-tuple-element.54), channel_id=1, source_target_pairs={{24,16},{26,18},{28,20},{30,22},{25,17},{27,19},{29,21},{31,23}} | collective-permute-start | bytes 884744 | tf_op jit(solution)/shard_map/ppermute | solution.py:53
  523.3 57.6 %collective-permute-start.37 = (bf16[576,256]{1,0:T(8,128)(2,1)}, bf16[576,256]{1,0:T(8,128)(2,1)}, u32[]{:S(2)}, u32[]{:S(2)}) collective-permute-start(bf16[576,256]{1,0:T(8,128)(2,1)} %fusion.41), channel_id=1, source_target_pairs={{0,8},{2,10},{4,12},{6,14},{8,16},{10,18},{12,20},{14,22},{1,9},{3... | collective-permute-start | bytes 884744 | tf_op jit(solution)/shard_map/ppermute | solution.py:52
  525.3 57.4 %collective-permute-start.42 = (bf16[4,576,256]{2,1,0:T(8,128)(2,1)S(1)}, bf16[4,576,256]{2,1,0:T(8,128)(2,1)}, u32[]{:S(2)}, u32[]{:S(2)}) collective-permute-start(bf16[4,576,256]{2,1,0:T(8,128)(2,1)S(1)} %fusion.12), channel_id=1, source_target_pairs={{0,4},{2,6},{4,0},{6,2},{8,12},{10,14},{12,8},{14,10},{16,20},{18,... | collective-permute-start | bytes 3538952 | tf_op jit(solution)/shard_map/ppermute | solution.py:184
  579.3 27.5 %collective-permute-start.32 = (bf16[576,384]{1,0:T(8,128)(2,1)S(1)}, bf16[576,384]{1,0:T(8,128)(2,1)S(1)}, u32[]{:S(2)}, u32[]{:S(2)}) collective-permute-start(bf16[576,384]{1,0:T(8,128)(2,1)S(1)} %get-tuple-element.50), channel_id=1, source_target_pairs={{24,16},{26,18},{28,20},{30,22},{25,17},{27,19},{29,21},{31,23}} | collective-permute-start | bytes 1327112 | tf_op jit(solution)/shard_map/ppermute | solution.py:53
  580.2 45.4 %collective-permute-start.28 = (bf16[1024,1024]{0,1:T(8,128)(2,1)S(1)}, bf16[1024,1024]{0,1:T(8,128)(2,1)S(1)}, u32[]{:S(2)}, u32[]{:S(2)}) collective-permute-start(bf16[1024,1024]{0,1:T(8,128)(2,1)S(1)} %pad_maximum_fusion.2), channel_id=1, source_target_pairs={{0,2},{2,0},{4,6},{6,4},{8,10},{10,8},{12,14},{14,12},{16,18},{18,... | collective-permute-start | bytes 6291464 | tf_op jit(solution)/shard_map/ppermute | solution.py:190
  615.5 28.2 %collective-permute-start.31 = (bf16[576,384]{1,0:T(8,128)(2,1)S(1)}, bf16[576,384]{1,0:T(8,128)(2,1)S(1)}, u32[]{:S(2)}, u32[]{:S(2)}) collective-permute-start(bf16[576,384]{1,0:T(8,128)(2,1)S(1)} %get-tuple-element.47), channel_id=1, source_target_pairs={{0,8},{2,10},{4,12},{6,14},{8,16},{10,18},{12,20},{14,22},{16,24},... | collective-permute-start | bytes 1327112 | tf_op jit(solution)/shard_map/ppermute | solution.py:52
  (59 other events, 752.2 us)
Sparse Core Ops, SparseCore 0:
  33.5 19.9 all-gather.2
  262.5 25.9 all-gather.4

commit v4 on v3

--- a/solution.py
+++ b/solution.py
@@ -6,7 +6,7 @@
 eta_scale = 2.0
 NX = 2
 NY = 2
-CHUNKS = (3, 2, 2, 1)
+CHUNKS = (1, 1, 1, 1)
 
 
 def x_pairs(n):
@@ -102,7 +102,6 @@
     half = attn_out.shape[1] // NX
     rows_out = w_out.shape[0]
 
-    grad_other = lax.ppermute(grad_out, "dp", x_pairs(n))
     features = lax.all_gather(grad_out, "tensor", axis=1, tiled=True)
     attn_mine = lax.dynamic_slice_in_dim(attn_out, x * half, half, 1)
     attn_send = lax.dynamic_slice_in_dim(attn_out, (1 - x) * half, half, 1)
@@ -122,9 +121,6 @@
     keep = line_reduce(keep + got, z, n, jnp.float32)
     last = lax.ppermute(at(keep, 1 - x), "dp", x_pairs(n))
     both = at(keep, x) + last
-    features_other = lax.all_gather(after(grad_other, last), "tensor", axis=1, tiled=True)
-    attn_other = lax.ppermute(after(attn_send, last), "dp", x_pairs(n))
-    attn_both = jnp.concatenate([attn_mine, attn_other], axis=0)
     upper, lower = both[:, 0], both[:, 1]
 
     base = (jnp.arange(prompts_dev, dtype=jnp.int32) * groups)[:, None]
@@ -150,18 +146,22 @@
         shaped = block.astype(jnp.float32).reshape(resp_dev, -1, width)
         return (shaped * by[:, None, None]).reshape(block.shape).astype(jnp.bfloat16)
 
-    weighted = jnp.concatenate([scale(features, coef), scale(features_other, coef_other)], axis=0)
-
     w_send = lax.dynamic_slice_in_dim(w_out, (1 - x) * half, half, 1)
     w_other = lax.ppermute(after(w_send, send), "dp", x_pairs(n))
+    grad_other = lax.ppermute(after(grad_out, w_other), "dp", x_pairs(n))
     w_mine = lax.dynamic_slice_in_dim(w_out, x * half, half, 1)
     w_pair = in_order(x == 0, w_mine, w_other, 0)
     w_a, w_b = w_pair[:, : half // 2], w_pair[:, half // 2 :]
     w_a = line_gather(w_a, z, n)
-    w_a_other = lax.ppermute(after(w_a, got), "dp", y_pairs(n))
+    w_b_other = lax.ppermute(after(w_b, got), "dp", y_pairs(n))
+    w_a_other = lax.ppermute(after(w_a, w_b_other), "dp", y_pairs(n))
     w_a = in_order(y == 0, w_a[:, None], w_a_other[:, None], 1).reshape(-1, half // 2)
-    w_b_other = lax.ppermute(after(w_b, got), "dp", y_pairs(n))
     w_b = in_order(y == 0, w_b[None], w_b_other[None], 0)
+
+    features_other = lax.all_gather(after(grad_other, last), "tensor", axis=1, tiled=True)
+    attn_other = lax.ppermute(after(attn_send, last), "dp", x_pairs(n))
+    attn_both = jnp.concatenate([attn_mine, attn_other], axis=0)
+    weighted = jnp.concatenate([scale(features, coef), scale(features_other, coef_other)], axis=0)
 
     unit = half // sum(CHUNKS)
     pieces = []
@@ -179,8 +179,8 @@
         mine = lax.dynamic_index_in_dim(block, y, 1, keepdims=False)
         away = lax.dynamic_index_in_dim(block, 1 - y, 1, keepdims=False).astype(jnp.bfloat16)
         begin += step
-        if c >= 2:
-            away = after(away, arrivals[c - 2])
+        if c >= 1:
+            away = after(away, arrivals[c - 1])
         came = lax.ppermute(away, "dp", y_pairs(n))
         arrivals.append(came)
         if c == 0:

time: 691 us -> 675 us (0.977)
  waiting for transfers between devices: 325 us -> 297 us
  starting transfers between devices: 127 us -> 138 us
  matrix products: 79.8 us -> 72.8 us
    ppermute x4, waiting for transfers between devices: 39.8 us -> 6.85 us  [shards(): came = lax.ppermute(away, 'dp', y_pairs(n))]
    ppermute x1, waiting for transfers between devices: 3.74 us -> 20.5 us  [shards(): lax.ppermute(project(weighted[tokens:], w_a, w_b), 'dp', x_pairs(n))]
    ppermute x15, starting transfers between devices: 55.7 us -> 64.4 us  [line_reduce(): right = lax.ppermute(give_r.astype(dtype), 'dp', z_pairs(n, step, 1, False))]
    unnamed x61 -> x65, local copies, waits for them, and re-layouts: 30.9 us -> 30 us
where the time goes in v4:
time: 675 us; the launch traced here: 665 us
  waiting for transfers between devices  297 us (44%)
  starting transfers between devices  138 us (20%)
  matrix products  72.8 us (11%)
  local copies, waits for them, and re-layouts  70.3 us (10%)
  other arithmetic  68.6 us (10%)
  between operations  15.2 us (2%)
    ppermute x1, waiting for transfers between devices, shards(): w_other = lax.ppermute(after(w_send, send), 'dp', x_pairs(n))  96.9 us
    ppermute x15, starting transfers between devices, line_reduce(): right = lax.ppermute(give_r.astype(dtype), 'dp', z_pairs(n, step, 1, False))  64.4 us
    ppermute x1, waiting for transfers between devices, shards(): got = lax.ppermute(send, 'dp', y_pairs(n))  50.3 us
    ppermute x1, waiting for transfers between devices, shards(): w_b_other = lax.ppermute(after(w_b, got), 'dp', y_pairs(n))  49.9 us
    dot_general x4, matrix products, shards(): lax.dot_general(weighted, attn_both[:, begin:begin + step], (((0,), (0,))...  39.5 us
    dot_general x4, matrix products, project(): jnp.dot(block, part, preferred_element_type=jnp.float32)  30.3 us
    unnamed x65, local copies, waits for them, and re-layouts  30 us
    ppermute x6, starting transfers between devices, line_gather(): right = lax.ppermute(right, 'dp', z_pairs(n, step, 1, True))  26.6 us
  transfers between devices with their start and end apart: 59, of which 21 were waited for; matrix products, arithmetic and copies ran while one was open for 29% of the time, Pallas kernels for 0%

profile of v4, /device:TPU:0, one launch (start us, length us, event | category | flops | bytes accessed | tf_op | source)
XLA Modules:
  0.0 664.5 jit_solution(13717624531225996943)
XLA Ops:
  9.1 8.3 %all-to-all-start = ((bf16[16,16,288]{2,1,0:T(8,128)(2,1)}), bf16[16,16,288]{2,1,0:T(8,128)(2,1)S(1)}, u32[]{:S(2)}, u32[]{:S(2)}) async-start(bf16[16,16,288]{2,1,0:T(8,128)(2,1)} %bitcast.243), calls=%async_computation | async-start | bytes 393216 | tf_op jit(solution)/shard_map/all_to_all | solution.py:110
  17.5 8.5 %all-to-all-done = bf16[16,16,288]{2,1,0:T(8,128)(2,1)S(1)} async-done(((bf16[16,16,288]{2,1,0:T(8,128)(2,1)}), bf16[16,16,288]{2,1,0:T(8,128)(2,1)S(1)}, u32[]{:S(2)}, u32[]{:S(2)}) %all-to-all-start) | async-done | bytes 147488 | tf_op jit(solution)/shard_map/all_to_all | solution.py:110
  33.4 50.3 %collective-permute-done = f32[4,2,16,2,2304]{4,2,3,1,0:T(8,128)S(1)} collective-permute-done((f32[4,2,16,2,2304]{4,2,3,1,0:T(8,128)}, f32[4,2,16,2,2304]{4,2,3,1,0:T(8,128)S(1)}, u32[]{:S(2)}, u32[]{:S(2)}) %collective-permute-start) | collective-permute-done | bytes 2359328 | tf_op jit(solution)/shard_map/ppermute | solution.py:120
  108.6 96.9 %collective-permute-done.12 = bf16[288,1024]{1,0:T(8,128)(2,1)S(1)} collective-permute-done((bf16[288,1024]{1,0:T(8,128)(2,1)}, bf16[288,1024]{1,0:T(8,128)(2,1)S(1)}, u32[]{:S(2)}, u32[]{:S(2)}) %collective-permute-start.12) | collective-permute-done | bytes 589856 | tf_op jit(solution)/shard_map/ppermute | solution.py:150
  221.4 11.2 %collective-permute-start.3 = (f32[2,16,2,2304]{3,1,2,0:T(8,128)}, f32[2,16,2,2304]{3,1,2,0:T(8,128)}, u32[]{:S(2)}, u32[]{:S(2)}) collective-permute-start(f32[2,16,2,2304]{3,1,2,0:T(8,128)} %get-tuple-element.59), channel_id=1, source_target_pairs={{0,8},{2,10},{4,12},{6,14},{8,16},{10,18},{12,20},{14,22},{16,24},... | collective-permute-start | bytes 1769480 | tf_op jit(solution)/shard_map/ppermute | solution.py:52
  241.2 11.6 %collective-permute-done.6 = f32[2,16,2,2304]{3,1,2,0:T(8,128)} collective-permute-done((f32[2,16,2,2304]{3,1,2,0:T(8,128)}, f32[2,16,2,2304]{3,1,2,0:T(8,128)}, u32[]{:S(2)}, u32[]{:S(2)}) %collective-permute-start.6) | collective-permute-done | bytes 589856 | tf_op jit(solution)/shard_map/ppermute | solution.py:53
  269.1 11.4 %collective-permute-done.18 = bf16[576,512]{1,0:T(8,128)(2,1)S(1)} collective-permute-done((bf16[576,512]{1,0:T(8,128)(2,1)}, bf16[576,512]{1,0:T(8,128)(2,1)S(1)}, u32[]{:S(2)}, u32[]{:S(2)}) %collective-permute-start.18) | collective-permute-done | bytes 589856 | tf_op jit(solution)/shard_map/ppermute | solution.py:63
  295.5 49.9 %collective-permute-done.21 = bf16[576,512]{1,0:T(8,128)(2,1)S(1)} collective-permute-done((bf16[576,512]{1,0:T(8,128)(2,1)S(1)}, bf16[576,512]{1,0:T(8,128)(2,1)S(1)}, u32[]{:S(2)}, u32[]{:S(2)}) %collective-permute-start.21) | collective-permute-done | bytes 589856 | tf_op jit(solution)/shard_map/ppermute | solution.py:156
  371.4 14.2 %collective-permute-start.23 = (bf16[2,576,512]{2,1,0:T(8,128)(2,1)}, bf16[2,576,512]{2,1,0:T(8,128)(2,1)}, u32[]{:S(2)}, u32[]{:S(2)}) collective-permute-start(bf16[2,576,512]{2,1,0:T(8,128)(2,1)} %collective-permute-done.22), channel_id=1, source_target_pairs={{8,16},{10,18},{12,20},{14,22},{16,24},{18,26},{20,28},{22,30},{9,... | collective-permute-start | bytes 3538952 | tf_op jit(solution)/shard_map/ppermute | solution.py:62
  385.8 10.4 %multiply_convert_fusion.1 = bf16[1024,4608]{1,0:T(8,128)(2,1)} fusion(bf16[1024,4608]{1,0:T(8,128)(2,1)} %all-gather.3.cloned.1.call-done, f32[1024]{0:T(1024)S(1)} %mul.130), kind=kLoop, calls=%fused_computation.6 | loop fusion | flops 14155776 | bytes 18878464 | tf_op jit(solution)/shard_map/convert_element_type | solution.py:147
  402.7 10.7 %multiply_convert_fusion = bf16[1024,4608]{1,0:T(8,128)(2,1)} fusion(bf16[1024,4608]{1,0:T(8,128)(2,1)} %all-gather.5.cloned.1.call-done, f32[1024]{0:T(1024)S(1)} %mul.134), kind=kLoop, calls=%fused_computation.5 | loop fusion | flops 14155776 | bytes 18878464 | tf_op jit(solution)/shard_map/convert_element_type | solution.py:147
  417.5 11.0 %fusion.18 = f32[4608,256]{1,0:T(8,128)} fusion(bf16[1024,1024]{1,0:T(8,128)(2,1)} %get-tuple-element.42, bf16[1024,1024]{1,0:T(8,128)(2,1)} %collective-permute-done.10, bf16[1024,4608]{1,0:T(8,128)(2,1)} %multiply_convert_fusion, bf16[1024,4608]{1,0:T(8,128)(2,1)} %multiply_convert_fusion.1), kind=kOutput, calls=%fused_computation.66 | convolution fusion | flops 4871684096 | bytes 27787264 | tf_op jit(solution)/shard_map/dot_general | solution.py:173
  431.6 9.5 %fusion.20 = f32[4608,256]{1,0:T(8,128)} fusion(bf16[1024,1024]{1,0:T(8,128)(2,1)} %collective-permute-done.10, bf16[1024,1024]{1,0:T(8,128)(2,1)} %get-tuple-element.42, bf16[1024,4608]{1,0:T(8,128)(2,1)} %multiply_convert_fusion, bf16[1024,4608]{1,0:T(8,128)(2,1)S(1)} %bitcast.245), kind=kOutput, calls=%fused_computation.68 | convolution fusion | flops 4871684096 | bytes 27787264 | tf_op jit(solution)/shard_map/dot_general | solution.py:173
  445.6 9.5 %fusion.12 = f32[4608,256]{1,0:T(8,128)} fusion(bf16[1024,1024]{1,0:T(8,128)(2,1)} %get-tuple-element.42, bf16[1024,1024]{1,0:T(8,128)(2,1)} %collective-permute-done.10, bf16[1024,4608]{1,0:T(8,128)(2,1)} %multiply_convert_fusion, bf16[1024,4608]{1,0:T(8,128)(2,1)S(1)} %bitcast.245), kind=kOutput, calls=%fused_computation.62 | convolution fusion | flops 4871684096 | bytes 27787264 | tf_op jit(solution)/shard_map/dot_general | solution.py:173
  455.1 9.5 %fusion.15 = f32[4608,256]{1,0:T(8,128)} fusion(bf16[1024,1024]{1,0:T(8,128)(2,1)} %get-tuple-element.42, bf16[1024,1024]{1,0:T(8,128)(2,1)} %collective-permute-done.10, bf16[1024,4608]{1,0:T(8,128)(2,1)} %multiply_convert_fusion, bf16[1024,4608]{1,0:T(8,128)(2,1)S(1)} %bitcast.245), kind=kOutput, calls=%fused_computation.64 | convolution fusion | flops 4871684096 | bytes 27787264 | tf_op jit(solution)/shard_map/dot_general | solution.py:173
  476.9 6.8 %collective-permute-done.42 = bf16[4,576,256]{2,1,0:T(8,128)(2,1)} collective-permute-done((bf16[4,576,256]{2,1,0:T(8,128)(2,1)}, bf16[4,576,256]{2,1,0:T(8,128)(2,1)}, u32[]{:S(2)}, u32[]{:S(2)}) %collective-permute-start.42) | collective-permute-done | bytes 1179680 | tf_op jit(solution)/shard_map/ppermute | solution.py:184
  487.3 6.2 convolution_convert_fusion.3
  495.5 8.9 %convolution_convert_fusion.1 = bf16[1024,512]{0,1:T(8,128)(2,1)} fusion(bf16[1024,4608]{1,0:T(8,128)(2,1)} %multiply_convert_fusion, bf16[4608,512]{1,0:T(8,128)(2,1)S(1)} %bitcast.251), kind=kOutput, calls=%fused_computation.39 | convolution fusion | flops 4832362496 | bytes 15204352 | tf_op jit(solution)/shard_map/dot_general | solution.py:83
  523.3 9.0 %convolution_convert_fusion = bf16[1024,512]{0,1:T(8,128)(2,1)} fusion(bf16[1024,4608]{1,0:T(8,128)(2,1)} %multiply_convert_fusion, bf16[4608,512]{1,0:T(8,128)(2,1)S(1)} %bitcast.252), kind=kOutput, calls=%fused_computation.38 | convolution fusion | flops 4832362496 | bytes 15204352 | tf_op jit(solution)/shard_map/dot_general | solution.py:83
  544.1 6.2 convolution_convert_fusion.2
  560.3 20.5 %collective-permute-done.28 = bf16[1024,1024]{0,1:T(8,128)(2,1)} collective-permute-done((bf16[1024,1024]{0,1:T(8,128)(2,1)}, bf16[1024,1024]{0,1:T(8,128)(2,1)}, u32[]{:S(2)}, u32[]{:S(2)}) %collective-permute-start.28) | collective-permute-done | bytes 2097184 | tf_op jit(solution)/shard_map/ppermute | solution.py:190
  612.0 6.7 %collective-permute-start.38 = (bf16[576,256]{1,0:T(8,128)(2,1)S(1)}, bf16[576,256]{1,0:T(8,128)(2,1)S(1)}, u32[]{:S(2)}, u32[]{:S(2)}) collective-permute-start(bf16[576,256]{1,0:T(8,128)(2,1)S(1)} %get-tuple-element.47), channel_id=1, source_target_pairs={{0,8},{2,10},{4,12},{6,14},{8,16},{10,18},{12,20},{14,22},{16,24},... | collective-permute-start | bytes 884744 | tf_op jit(solution)/shard_map/ppermute | solution.py:52
  620.1 16.1 %collective-permute-start.51 = (bf16[576,256]{1,0:T(8,128)(2,1)S(1)}, bf16[576,256]{1,0:T(8,128)(2,1)S(1)}, u32[]{:S(2)}, u32[]{:S(2)}) collective-permute-start(bf16[576,256]{1,0:T(8,128)(2,1)S(1)} %get-tuple-element.55), channel_id=1, source_target_pairs={{0,8},{2,10},{4,12},{6,14},{8,16},{10,18},{12,20},{14,22},{16,24},... | collective-permute-start | bytes 884744 | tf_op jit(solution)/shard_map/ppermute | solution.py:52
  646.5 6.4 copy.35
  (267 shorter events, 239.3 us)
Async XLA Ops:
  17.4 368.4 %all-gather.3.cloned.1.call-start = ((), (), s32[]{:S(2)}) async-start(), calls=%async_computation.1 | async-start | bytes 14155776 | tf_op jit(solution)/shard_map/all_gather | solution.py:105
  32.5 51.3 %collective-permute-start = (f32[4,2,16,2,2304]{4,2,3,1,0:T(8,128)}, f32[4,2,16,2,2304]{4,2,3,1,0:T(8,128)S(1)}, u32[]{:S(2)}, u32[]{:S(2)}) collective-permute-start(f32[4,2,16,2,2304]{4,2,3,1,0:T(8,128)} %bitcast.242), channel_id=1, source_target_pairs={{0,4},{2,6},{4,0},{6,2},{8,12},{10,14},{12,8},{14,10},{16,20},{18,... | collective-permute-start | bytes 7077896 | tf_op jit(solution)/shard_map/ppermute | solution.py:120
  33.3 369.4 %all-gather.5.cloned.1.call-start = ((), (), s32[]{:S(2)}) async-start(), calls=%async_computation.2 | async-start | bytes 14155776 | tf_op jit(solution)/shard_map/all_gather | solution.py:161
  92.4 169.8 %collective-permute-start.8 = (bf16[1024,2304]{1,0:T(8,128)(2,1)}, bf16[1024,2304]{1,0:T(8,128)(2,1)}, u32[]{:S(2)}, u32[]{:S(2)}) collective-permute-start(bf16[1024,2304]{1,0:T(8,128)(2,1)} %param.20), channel_id=1, source_target_pairs={{0,2},{2,0},{4,6},{6,4},{8,10},{10,8},{12,14},{14,12},{16,18},{18,... | collective-permute-start | bytes 14155784 | tf_op jit(solution)/shard_map/ppermute | solution.py:151
  94.1 111.4 %collective-permute-start.12 = (bf16[288,1024]{1,0:T(8,128)(2,1)}, bf16[288,1024]{1,0:T(8,128)(2,1)S(1)}, u32[]{:S(2)}, u32[]{:S(2)}) collective-permute-start(bf16[288,1024]{1,0:T(8,128)(2,1)} %get-tuple-element.67), channel_id=1, source_target_pairs={{0,2},{2,0},{4,6},{6,4},{8,10},{10,8},{12,14},{14,12},{16,18},{18,... | collective-permute-start | bytes 1769480 | tf_op jit(solution)/shard_map/ppermute | solution.py:150
  95.5 116.3 %collective-permute-start.4 = (f32[2,16,2,2304]{3,1,2,0:T(8,128)}, f32[2,16,2,2304]{3,1,2,0:T(8,128)}, u32[]{:S(2)}, u32[]{:S(2)}) collective-permute-start(f32[2,16,2,2304]{3,1,2,0:T(8,128)} %get-tuple-element.62), channel_id=1, source_target_pairs={{24,16},{26,18},{28,20},{30,22},{25,17},{27,19},{29,21},{31,23}} | collective-permute-start | bytes 1769480 | tf_op jit(solution)/shard_map/ppermute | solution.py:53
  103.4 108.5 %collective-permute-start.2 = (f32[2,16,2,2304]{3,1,2,0:T(8,128)}, f32[2,16,2,2304]{3,1,2,0:T(8,128)}, u32[]{:S(2)}, u32[]{:S(2)}) collective-permute-start(f32[2,16,2,2304]{3,1,2,0:T(8,128)} %bitcast_add_fusion.27), channel_id=1, source_target_pairs={{0,8},{2,10},{4,12},{6,14},{8,16},{10,18},{12,20},{14,22},{1,9},{3... | collective-permute-start | bytes 1769480 | tf_op jit(solution)/shard_map/ppermute | solution.py:52
  284.0 68.7 %collective-permute-start.19 = (bf16[4,576,512]{2,1,0:T(8,128)(2,1)}, bf16[4,576,512]{2,1,0:T(8,128)(2,1)}, u32[]{:S(2)}, u32[]{:S(2)}) collective-permute-start(bf16[4,576,512]{2,1,0:T(8,128)(2,1)} %constant_dynamic-slice_fusion.1), channel_id=1, source_target_pairs={{0,4},{2,6},{4,0},{6,2},{8,12},{10,14},{12,8},{14,10},{16,20},{18,... | collective-permute-start | bytes 7077896 | tf_op jit(solution)/shard_map/ppermute | solution.py:157
  289.3 56.2 %collective-permute-start.21 = (bf16[576,512]{1,0:T(8,128)(2,1)S(1)}, bf16[576,512]{1,0:T(8,128)(2,1)S(1)}, u32[]{:S(2)}, u32[]{:S(2)}) collective-permute-start(bf16[576,512]{1,0:T(8,128)(2,1)S(1)} %copy-done.13), channel_id=1, source_target_pairs={{0,4},{2,6},{4,0},{6,2},{8,12},{10,14},{12,8},{14,10},{16,20},{18,... | collective-permute-start | bytes 1769480 | tf_op jit(solution)/shard_map/ppermute | solution.py:156
  369.8 47.7 %collective-permute-start.10 = (bf16[1024,1024]{1,0:T(8,128)(2,1)}, bf16[1024,1024]{1,0:T(8,128)(2,1)}, u32[]{:S(2)}, u32[]{:S(2)}) collective-permute-start(bf16[1024,1024]{1,0:T(8,128)(2,1)} %get-tuple-element.16), channel_id=1, source_target_pairs={{0,2},{2,0},{4,6},{6,4},{8,10},{10,8},{12,14},{14,12},{16,18},{18,... | collective-permute-start | bytes 6291464 | tf_op jit(solution)/shard_map/ppermute | solution.py:162
  399.7 93.8 %collective-permute-start.27 = (bf16[2,576,512]{2,1,0:T(8,128)(2,1)}, bf16[2,576,512]{2,1,0:T(8,128)(2,1)}, u32[]{:S(2)}, u32[]{:S(2)}) collective-permute-start(bf16[2,576,512]{2,1,0:T(8,128)(2,1)} %collective-permute-done.26), channel_id=1, source_target_pairs={{8,0},{10,2},{12,4},{14,6},{9,1},{11,3},{13,5},{15,7}} | collective-permute-start | bytes 3538952 | tf_op jit(solution)/shard_map/ppermute | solution.py:63
  401.0 103.3 %collective-permute-start.24 = (bf16[2,576,512]{2,1,0:T(8,128)(2,1)}, bf16[2,576,512]{2,1,0:T(8,128)(2,1)}, u32[]{:S(2)}, u32[]{:S(2)}) collective-permute-start(bf16[2,576,512]{2,1,0:T(8,128)(2,1)} %collective-permute-done.23), channel_id=1, source_target_pairs={{16,24},{18,26},{20,28},{22,30},{17,25},{19,27},{21,29},{23,31}} | collective-permute-start | bytes 3538952 | tf_op jit(solution)/shard_map/ppermute | solution.py:62
  431.3 39.1 %collective-permute-start.20 = (bf16[4,576,256]{2,1,0:T(8,128)(2,1)}, bf16[4,576,256]{2,1,0:T(8,128)(2,1)}, u32[]{:S(2)}, u32[]{:S(2)}) collective-permute-start(bf16[4,576,256]{2,1,0:T(8,128)(2,1)} %fusion.8), channel_id=1, source_target_pairs={{0,4},{2,6},{4,0},{6,2},{8,12},{10,14},{12,8},{14,10},{16,20},{18,... | collective-permute-start | bytes 3538952 | tf_op jit(solution)/shard_map/ppermute | solution.py:184
  443.9 39.9 %collective-permute-start.42 = (bf16[4,576,256]{2,1,0:T(8,128)(2,1)}, bf16[4,576,256]{2,1,0:T(8,128)(2,1)}, u32[]{:S(2)}, u32[]{:S(2)}) collective-permute-start(bf16[4,576,256]{2,1,0:T(8,128)(2,1)} %fusion.10), channel_id=1, source_target_pairs={{0,4},{2,6},{4,0},{6,2},{8,12},{10,14},{12,8},{14,10},{16,20},{18,... | collective-permute-start | bytes 3538952 | tf_op jit(solution)/shard_map/ppermute | solution.py:184
  473.7 61.4 %collective-permute-start.29 = (bf16[576,256]{1,0:T(8,128)(2,1)}, bf16[576,256]{1,0:T(8,128)(2,1)}, u32[]{:S(2)}, u32[]{:S(2)}) collective-permute-start(bf16[576,256]{1,0:T(8,128)(2,1)} %get-tuple-element.45), channel_id=1, source_target_pairs={{0,8},{2,10},{4,12},{6,14},{1,9},{3,11},{5,13},{7,15}} | collective-permute-start | bytes 884744 | tf_op jit(solution)/shard_map/ppermute | solution.py:52
  476.3 65.6 %collective-permute-start.32 = (bf16[576,256]{1,0:T(8,128)(2,1)}, bf16[576,256]{1,0:T(8,128)(2,1)S(1)}, u32[]{:S(2)}, u32[]{:S(2)}) collective-permute-start(bf16[576,256]{1,0:T(8,128)(2,1)} %get-tuple-element.46), channel_id=1, source_target_pairs={{24,16},{26,18},{28,20},{30,22},{25,17},{27,19},{29,21},{31,23}} | collective-permute-start | bytes 884744 | tf_op jit(solution)/shard_map/ppermute | solution.py:53
  483.8 73.1 %collective-permute-start.35 = (bf16[4,576,256]{2,1,0:T(8,128)(2,1)}, bf16[4,576,256]{2,1,0:T(8,128)(2,1)}, u32[]{:S(2)}, u32[]{:S(2)}) collective-permute-start(bf16[4,576,256]{2,1,0:T(8,128)(2,1)} %fusion.9), channel_id=1, source_target_pairs={{0,4},{2,6},{4,0},{6,2},{8,12},{10,14},{12,8},{14,10},{16,20},{18,... | collective-permute-start | bytes 3538952 | tf_op jit(solution)/shard_map/ppermute | solution.py:184
  493.5 44.4 %collective-permute-start.43 = (bf16[576,256]{1,0:T(8,128)(2,1)}, bf16[576,256]{1,0:T(8,128)(2,1)}, u32[]{:S(2)}, u32[]{:S(2)}) collective-permute-start(bf16[576,256]{1,0:T(8,128)(2,1)} %get-tuple-element.53), channel_id=1, source_target_pairs={{0,8},{2,10},{4,12},{6,14},{1,9},{3,11},{5,13},{7,15}} | collective-permute-start | bytes 884744 | tf_op jit(solution)/shard_map/ppermute | solution.py:52
  504.4 48.8 %collective-permute-start.46 = (bf16[576,256]{1,0:T(8,128)(2,1)}, bf16[576,256]{1,0:T(8,128)(2,1)S(1)}, u32[]{:S(2)}, u32[]{:S(2)}) collective-permute-start(bf16[576,256]{1,0:T(8,128)(2,1)} %get-tuple-element.54), channel_id=1, source_target_pairs={{24,16},{26,18},{28,20},{30,22},{25,17},{27,19},{29,21},{31,23}} | collective-permute-start | bytes 884744 | tf_op jit(solution)/shard_map/ppermute | solution.py:53
  535.1 45.7 %collective-permute-start.28 = (bf16[1024,1024]{0,1:T(8,128)(2,1)}, bf16[1024,1024]{0,1:T(8,128)(2,1)}, u32[]{:S(2)}, u32[]{:S(2)}) collective-permute-start(bf16[1024,1024]{0,1:T(8,128)(2,1)} %pad_maximum_fusion.2), channel_id=1, source_target_pairs={{0,2},{2,0},{4,6},{6,4},{8,10},{10,8},{12,14},{14,12},{16,18},{18,... | collective-permute-start | bytes 6291464 | tf_op jit(solution)/shard_map/ppermute | solution.py:190
  550.3 36.8 %collective-permute-start.11 = (bf16[4,576,256]{2,1,0:T(8,128)(2,1)S(1)}, bf16[4,576,256]{2,1,0:T(8,128)(2,1)S(1)}, u32[]{:S(2)}, u32[]{:S(2)}) collective-permute-start(bf16[4,576,256]{2,1,0:T(8,128)(2,1)S(1)} %copy-done.7), channel_id=1, source_target_pairs={{0,4},{2,6},{4,0},{6,2},{8,12},{10,14},{12,8},{14,10},{16,20},{18,... | collective-permute-start | bytes 3538952 | tf_op jit(solution)/shard_map/ppermute | solution.py:184
  553.2 35.5 %collective-permute-start.33 = (bf16[576,256]{1,0:T(8,128)(2,1)S(1)}, bf16[576,256]{1,0:T(8,128)(2,1)S(1)}, u32[]{:S(2)}, u32[]{:S(2)}) collective-permute-start(bf16[576,256]{1,0:T(8,128)(2,1)S(1)} %get-tuple-element.44), channel_id=1, source_target_pairs={{16,8},{18,10},{20,12},{22,14},{24,16},{26,18},{28,20},{30,22},{17... | collective-permute-start | bytes 884744 | tf_op jit(solution)/shard_map/ppermute | solution.py:53
  553.9 55.5 %collective-permute-start.31 = (bf16[576,256]{1,0:T(8,128)(2,1)S(1)}, bf16[576,256]{1,0:T(8,128)(2,1)S(1)}, u32[]{:S(2)}, u32[]{:S(2)}) collective-permute-start(bf16[576,256]{1,0:T(8,128)(2,1)S(1)} %get-tuple-element.43), channel_id=1, source_target_pairs={{0,8},{2,10},{4,12},{6,14},{8,16},{10,18},{12,20},{14,22},{16,24},... | collective-permute-start | bytes 884744 | tf_op jit(solution)/shard_map/ppermute | solution.py:52
  556.9 39.9 %collective-permute-start.47 = (bf16[576,256]{1,0:T(8,128)(2,1)S(1)}, bf16[576,256]{1,0:T(8,128)(2,1)S(1)}, u32[]{:S(2)}, u32[]{:S(2)}) collective-permute-start(bf16[576,256]{1,0:T(8,128)(2,1)S(1)} %get-tuple-element.52), channel_id=1, source_target_pairs={{16,8},{18,10},{20,12},{22,14},{24,16},{26,18},{28,20},{30,22},{17... | collective-permute-start | bytes 884744 | tf_op jit(solution)/shard_map/ppermute | solution.py:53
  (61 other events, 971.9 us)
Sparse Core Ops, SparseCore 0:
  33.5 19.9 all-gather.2
  262.3 25.9 all-gather.4
